TPU v7x, 128 devices: a whole 4x4x4 slice. The times are simulated.
128 devices in a mesh: ctx: 8 (over y, core), head: 16 (over x, z).
Axes of the slice: x: 4, y: 4, z: 4, core: 2. Of those that a mesh axis runs over, the one named last changes fastest.
Arguments:
- queries: bfloat16 [4096, 16384], P('ctx', 'head'), may hold values from -8 to 8
- prompt_keys: bfloat16 [4096, 1024], P('ctx'), may hold values from -8 to 8
- prompt_values: bfloat16 [4096, 1024], P('ctx'), may hold values from -6 to 6
- owner_map: int32 [32, 8, 1], P('ctx'), may hold values from 0 to 15; in each aligned block of 32 rows (0 to 31, 32 to 63, ..., all dimensions but the last counted through in order) at most 4 rows name the same one
- head_layout: int32 [8], replicated, may hold values from 0 to 7, each once
- prompt_length: int32 [1], replicated, may hold values from 3840 to 4096
Outputs:
- attention: bfloat16 [4096, 16384], P('ctx', 'head')
- key_cache: bfloat16 [8, 64, 128, 128], P('ctx', 'head')
- value_cache: bfloat16 [8, 64, 128, 128], P('ctx', 'head')
- key_cache_scales: bfloat16 [8, 64], P('ctx', 'head')
- value_cache_scales: bfloat16 [8, 64], P('ctx', 'head')
Inputs may be any that keep to these rules, and one draw needn't show every extreme that they name: `owner_map`: among the 32 entries of one block of 4 pages no owner appears more than 4 times, and in every draw some owner of some block appears exactly 4 times. `head_layout`: each key-value head appears once. `prompt_length`: positions from the prompt length on are padding.
All inputs are finite; a program needn't handle non-finite values.
Results may differ from a plain program's by a relative error of at most 0.04.
Values may be sent and summed in bfloat16 or wider, within the bound.
A program may use at most 64 MiB of HBM per device.

v0:
```python
import math

import jax
import jax.numpy as jnp
from jax import lax
from jax.sharding import PartitionSpec as P

HD = 128
PAGE = 128


def passed_along(value, axis, steps):
    count = lax.axis_size(axis)
    initial, last = (max(0, -steps), min(count, count - steps))
    return lax.ppermute(value, axis, [(source, source + steps) for source in range(initial, last)])


def shortened(x):
    return jax.tree.map(lambda a: a.astype(jnp.bfloat16) if a.dtype == jnp.float32 else a, x)


def partner(x, axis, distance):
    return lax.ppermute(x, axis, [(i, i ^ 1 << distance) for i in range(lax.axis_size(axis))])


def hadamard(width):
    index_row = jnp.arange(width, dtype=jnp.int32)
    common = index_row[:, None] & index_row[None, :]
    parity = jnp.zeros((width, width), jnp.int32)
    for bit_level in range(width.bit_length() - 1):
        parity = parity + (common >> bit_level & 1)
    return (1.0 - 2.0 * (parity % 2).astype(jnp.float32)) / math.sqrt(width)


def quantize(rotated):
    largest = jnp.max(jnp.abs(rotated), axis=(1, 2))
    scales = (largest / 448.0 + 1e-06).astype(jnp.bfloat16)
    stored = (rotated / scales.astype(jnp.float32)[:, None, None]).astype(jnp.bfloat16)
    return (stored, scales)


def entry_slots(owners, head_layout, page_count, slot_count):
    kv_total = head_layout.shape[0]
    heads_range = jnp.arange(kv_total, dtype=jnp.int32)
    layout_rank = jnp.sum(
        heads_range[:, None] * (head_layout[:, None] == heads_range[None, :]).astype(jnp.int32),
        axis=0,
    )
    order_key = (
        layout_rank[None, :] * page_count + jnp.arange(page_count, dtype=jnp.int32)[:, None]
    ).reshape(-1)
    earlier = order_key[None, :] < order_key[:, None]
    same_owner = owners[..., :, None] == owners[..., None, :]
    slot_index = jnp.sum(jnp.logical_and(same_owner, earlier).astype(jnp.int32), axis=-1)
    return owners * slot_count + slot_index


def attend(softmax_state, kv_block, rotated_queries, positions, length, key_start):
    key_pages, value_pages, key_scale, value_scale = kv_block
    old_max, denominator, accumulated = softmax_state
    key_pos = key_start + jnp.arange(key_pages.shape[0], dtype=jnp.int32)
    key_cols = jnp.repeat(key_scale.astype(jnp.float32), PAGE)
    value_cols = jnp.repeat(value_scale.astype(jnp.float32), PAGE)
    scores = (
        jnp.einsum("qhd,kd->hqk", rotated_queries, key_pages, preferred_element_type=jnp.float32)
        * key_cols
        / math.sqrt(HD)
    )
    allowed = jnp.logical_and(
        jnp.logical_and(key_pos[None, :] <= positions[:, None], key_pos[None, :] < length),
        key_start >= 0,
    )
    masked = jnp.where(allowed[None], scores, -1e30)
    new_max = jnp.maximum(old_max, jnp.max(masked, axis=2))
    exp_scores = jnp.where(allowed[None], jnp.exp(masked - new_max[:, :, None]), 0.0)
    factor = jnp.exp(old_max - new_max)
    denominator = denominator * factor + jnp.sum(exp_scores, axis=2)
    weights = (exp_scores * value_cols).astype(jnp.bfloat16)
    accumulated = accumulated * factor[:, :, None] + jnp.einsum(
        "hqk,kd->hqd", weights, value_pages, preferred_element_type=jnp.float32
    )
    return (new_max, denominator, accumulated)


def per_device(queries, prompt_keys, prompt_values, owner_map, head_layout, prompt_length):
    ctx_count = lax.axis_size("ctx")
    head_count = lax.axis_size("head")
    ctx_index = lax.axis_index("ctx")
    head_index = lax.axis_index("head")
    tok_rows = queries.shape[0]
    local_heads = queries.shape[1] // HD
    kv_total = prompt_keys.shape[1] // HD
    sharing = head_count // kv_total
    kv_head = head_index // sharing
    member = head_index % sharing
    page_count = tok_rows // PAGE
    slot_count = 2 * kv_total * page_count // head_count
    share_rows = tok_rows // sharing
    share_pages = page_count // sharing
    length = prompt_length[0]
    rotation = hadamard(HD)
    positions = ctx_index * tok_rows + jnp.arange(tok_rows, dtype=jnp.int32)
    live_rows = positions < length

    def store_pages(source):
        column = lax.dynamic_slice_in_dim(source, kv_head * HD, HD, 1)
        kept_rows = jnp.where(live_rows[:, None], column.astype(jnp.float32), 0.0)
        rotated = jnp.dot(kept_rows, rotation, precision=lax.Precision.HIGHEST)
        stored, scales = quantize(rotated.reshape(page_count, PAGE, HD))
        return (stored, scales)

    key_stored, key_scale = store_pages(prompt_keys)
    value_stored, value_scale = store_pages(prompt_values)
    rotated_queries = jnp.einsum(
        "thd,de->the",
        queries.reshape(tok_rows, local_heads, HD).astype(jnp.float32),
        rotation,
        precision=lax.Precision.HIGHEST,
    ).astype(jnp.bfloat16)
    own_block = (
        key_stored.reshape(tok_rows, HD),
        value_stored.reshape(tok_rows, HD),
        key_scale,
        value_scale,
    )
    own_share = (
        lax.dynamic_slice_in_dim(own_block[0], member * share_rows, share_rows, 0),
        lax.dynamic_slice_in_dim(own_block[1], member * share_rows, share_rows, 0),
        lax.dynamic_slice_in_dim(key_scale, member * share_pages, share_pages, 0),
        lax.dynamic_slice_in_dim(value_scale, member * share_pages, share_pages, 0),
    )
    start_state = (
        jnp.full((local_heads, tok_rows), -1e30, jnp.float32),
        jnp.zeros((local_heads, tok_rows), jnp.float32),
        jnp.zeros((local_heads, tok_rows, HD), jnp.float32),
    )

    def run_block(state_in, kv_block, key_start):
        return attend(state_in, kv_block, rotated_queries, positions, length, key_start)

    first_state = attend(
        start_state, own_block, rotated_queries, positions, length, ctx_index * tok_rows
    )

    def parts_hop(hop_index, loop_carry):
        hop_state, kv_block = loop_carry
        cycle_part = (
            lax.dynamic_slice_in_dim(kv_block[0], member * share_rows, share_rows, 0),
            lax.dynamic_slice_in_dim(kv_block[1], member * share_rows, share_rows, 0),
            lax.dynamic_slice_in_dim(kv_block[2], member * share_pages, share_pages, 0),
            lax.dynamic_slice_in_dim(kv_block[3], member * share_pages, share_pages, 0),
        )
        cycle_part = passed_along(
            (cycle_part[0], cycle_part[1], cycle_part[2], cycle_part[3]), "ctx", 1
        )
        partner_part = jax.tree.map(
            lambda part, own: part.astype(own.dtype),
            partner(shortened(cycle_part), "head", 0),
            cycle_part,
        )
        upper_half = head_index >> 0 & 1 == 1
        cycle_part = tuple(
            (
                jnp.where(
                    upper_half,
                    jnp.concatenate([theirs_now, ours_now]),
                    jnp.concatenate([ours_now, theirs_now]),
                )
                for ours_now, theirs_now in zip(cycle_part, partner_part)
            )
        )
        return (run_block(hop_state, cycle_part, (ctx_index - hop_index) * tok_rows), cycle_part)

    softmax_state, last_block = lax.fori_loop(1, ctx_count, parts_hop, (first_state, own_block))
    rotated_out = softmax_state[2] / softmax_state[1][:, :, None]
    unrotated = jnp.einsum("hqd,de->qhe", rotated_out, rotation, precision=lax.Precision.HIGHEST)
    attention = (
        jnp.where(live_rows[:, None, None], unrotated, 0.0)
        .astype(jnp.bfloat16)
        .reshape(tok_rows, local_heads * HD)
    )
    outgoing = (
        lax.dynamic_slice_in_dim(key_stored, member * share_pages, share_pages, 0),
        lax.dynamic_slice_in_dim(value_stored, member * share_pages, share_pages, 0),
        own_share[2],
        own_share[3],
    )
    owners = owner_map[:, :, 0].reshape(-1)
    destination = entry_slots(owners, head_layout, page_count, slot_count)
    entries = page_count * kv_total
    arrived = (
        lax.all_gather(outgoing[0], "head", axis=0, tiled=True),
        lax.all_gather(outgoing[1], "head", axis=0, tiled=True),
        lax.all_gather(outgoing[2], "head", axis=0, tiled=True),
        lax.all_gather(outgoing[3], "head", axis=0, tiled=True),
    )
    piece_rows = arrived[0].shape[0]
    gathered_row = jnp.arange(piece_rows, dtype=jnp.int32)
    sender = gathered_row // share_pages
    local_page = sender % sharing * share_pages + gathered_row % share_pages
    entry_index = local_page * kv_total + sender // sharing
    picked = entry_index[:, None] == jnp.arange(entries, dtype=jnp.int32)[None, :]
    target = jnp.sum(jnp.where(picked, destination[None, :], 0), axis=1) - head_index * slot_count
    onehot = (target[:, None] == jnp.arange(slot_count, dtype=jnp.int32)[None, :]).astype(
        jnp.bfloat16
    )
    key_held = jnp.einsum("ns,npd->spd", onehot, arrived[0], preferred_element_type=jnp.float32)
    value_held = jnp.einsum("ns,npd->spd", onehot, arrived[1], preferred_element_type=jnp.float32)
    key_sums = jnp.dot(onehot.T, arrived[2], preferred_element_type=jnp.float32)
    value_sums = jnp.dot(onehot.T, arrived[3], preferred_element_type=jnp.float32)
    key_cache = key_held.astype(jnp.bfloat16)[None]
    value_cache = value_held.astype(jnp.bfloat16)[None]
    key_cache_scales = key_sums.astype(jnp.bfloat16)[None]
    value_cache_scales = value_sums.astype(jnp.bfloat16)[None]
    return (attention, key_cache, value_cache, key_cache_scales, value_cache_scales)


def solution(mesh):
    in_specs = (P("ctx", "head"), P("ctx", None), P("ctx", None), P("ctx", None, None), P(), P())
    out_specs = (
        P("ctx", "head"),
        P("ctx", "head", None, None),
        P("ctx", "head", None, None),
        P("ctx", "head"),
        P("ctx", "head"),
    )
    return jax.shard_map(
        per_device, mesh=mesh, in_specs=in_specs, out_specs=out_specs, check_vma=False
    )
```

profile of v0, /device:TPU:0, one launch (start us, length us, event | category | flops | bytes accessed | tf_op | source)
XLA Modules:
  0.0 293.7 jit_solution(15371582675356868354)
XLA Ops:
  20.9 3.2 %copy-done.1 = f32[512,512,8]{1,0,2:T(8,128)} copy-done((f32[512,512,8]{1,0,2:T(8,128)}, f32[512,512,8]{1,0,2:T(8,128)S(1)}, u32[]{:S(2)}) %copy-start.1) | copy-done | bytes 8388632
  28.3 42.2 %all-reduce.2 = (bf16[32]{0:T(256)(128)(2,1)S(1)}, bf16[32]{0:T(256)(128)(2,1)S(1)}) all-reduce(bf16[32]{0:T(256)(128)(2,1)S(1)} %dynamic-update-slice, bf16[32]{0:T(256)(128)(2,1)S(1)} %dynamic-update-slice.1), channel_id=1, replica_groups=mesh['ctx'=8,'head'=16] {'head'}, use_global_device_ids=true, to_apply=%add | all-reduce | flops 64 | bytes 256
  70.4 6.8 %fusion.16 = f32[8,512,128]{2,1,0:T(8,128)} fusion(f32[512,512,8]{1,0,2:T(8,128)} %copy-done.1, f32[512]{0:T(512)S(1)} %broadcast_bitcast_fusion.2, f32[8,512]{1,0:T(8,128)S(1)} %broadcast_maximum_fusion, f32[512]{0:T(512)S(1)} %broadcast_bitcast_fusion.3, pred[512,512]{0,1:T(8,128)(4,1)S(1)} %and_and_fusion.1, f32[8,512]{1,0:T(8,128)S(1)} %get-tuple-element.475, ...), kind=kOutput, calls=%fused_computation.37 | convolution fusion | flops 552075264 | bytes 10915840 | tf_op jit(solution)/shard_map/hqk,kd->hqd/dot_general | solution.py:79
  77.2 197.6 %while.28 = (s32[]{:T(128)}, f32[8,512]{1,0:T(8,128)S(1)}, f32[8,512]{1,0:T(8,128)S(1)}, f32[8,512,128]{2,1,0:T(8,128)}, bf16[512,128]{1,0:T(8,128)(2,1)S(1)}, /...) while((s32[]{:T(128)}, f32[8,512]{1,0:T(8,128)S(1)}, ...), condition=%wide.region_9.10_spmd.clone, body=%wide.region_6.9_spmd.clone.sunk | while | flops 1112418432 | bytes 50616080 | solution.py:174
  78.7 4.1 %collective-permute-start.4 = (bf16[2]{0:T(256)(128)(2,1)S(1)}, bf16[2]{0:T(256)(128)(2,1)S(1)}, u32[]{:S(2)}, u32[]{:S(2)}) collective-permute-start(bf16[2]{0:T(256)(128)(2,1)S(1)} %dynamic_slice.93), channel_id=1, source_target_pairs={{0,16},{16,32},{32,48},{48,64},{64,80},{80,96},{96,112},{1,17},{17... | collective-permute-start | bytes 20 | tf_op jit(solution)/shard_map/while/body/eval_jaxpr/ppermute | solution.py:15
  84.8 3.6 %collective-permute-start.6 = (bf16[256,128]{1,0:T(8,128)(2,1)S(1)}, bf16[256,128]{1,0:T(8,128)(2,1)S(1)}, u32[]{:S(2)}, u32[]{:S(2)}) collective-permute-start(bf16[256,128]{1,0:T(8,128)(2,1)S(1)} %constant_dynamic-slice_fusion.5), channel_id=1, source_target_pairs={{0,16},{16,32},{32,48},{48,64},{64,80},{80,96},{96,112},{1,17},{17... | collective-permute-start | bytes 196616 | tf_op jit(solution)/shard_map/while/body/eval_jaxpr/ppermute | solution.py:15
  95.3 3.2 %collective-permute-done.3 = bf16[256,128]{1,0:T(8,128)(2,1)S(1)} collective-permute-done((bf16[256,128]{1,0:T(8,128)(2,1)S(1)}, bf16[256,128]{1,0:T(8,128)(2,1)S(1)}, u32[]{:S(2)}, u32[]{:S(2)}) %collective-permute-start.3) | collective-permute-done | bytes 65568 | tf_op jit(solution)/shard_map/while/body/eval_jaxpr/ppermute | solution.py:23
  100.4 2.5 fusion.135
  103.0 3.7 %multiply_add_fusion.6 = f32[8,512,128]{2,1,0:T(8,128)S(1)} fusion(f32[8,512,128]{2,1,0:T(8,128)S(1)} %copy-done.3, f32[512,512,8]{1,0,2:T(8,128)S(1)} %get-tuple-element.596, f32[512]{0:T(512)S(1)} %broadcast_bitcast_fusion.7, f32[8,512]{1,0:T(8,128)S(1)} %max.11, f32[512]{0:T(512)S(1)} %broadcast_bitcast_fusion.6, ...), kind=kOutput, calls=%fused_computation.7.clone.1 | convolution fusion | flops 552599552 | bytes 13012992 | tf_op jit(solution)/shard_map/while/body/eval_jaxpr/hqk,kd->hqd/dot_general | solution.py:79
  109.5 4.0 %collective-permute-start.4 = (bf16[2]{0:T(256)(128)(2,1)S(1)}, bf16[2]{0:T(256)(128)(2,1)S(1)}, u32[]{:S(2)}, u32[]{:S(2)}) collective-permute-start(bf16[2]{0:T(256)(128)(2,1)S(1)} %dynamic_slice.93), channel_id=1, source_target_pairs={{0,16},{16,32},{32,48},{48,64},{64,80},{80,96},{96,112},{1,17},{17... | collective-permute-start | bytes 20 | tf_op jit(solution)/shard_map/while/body/eval_jaxpr/ppermute | solution.py:15
  130.0 2.5 fusion.135
  132.7 3.7 %multiply_add_fusion.6 = f32[8,512,128]{2,1,0:T(8,128)S(1)} fusion(f32[8,512,128]{2,1,0:T(8,128)S(1)} %copy-done.3, f32[512,512,8]{1,0,2:T(8,128)S(1)} %get-tuple-element.596, f32[512]{0:T(512)S(1)} %broadcast_bitcast_fusion.7, f32[8,512]{1,0:T(8,128)S(1)} %max.11, f32[512]{0:T(512)S(1)} %broadcast_bitcast_fusion.6, ...), kind=kOutput, calls=%fused_computation.7.clone.1 | convolution fusion | flops 552599552 | bytes 13012992 | tf_op jit(solution)/shard_map/while/body/eval_jaxpr/hqk,kd->hqd/dot_general | solution.py:79
  157.3 2.5 fusion.135
  159.9 3.7 %multiply_add_fusion.6 = f32[8,512,128]{2,1,0:T(8,128)S(1)} fusion(f32[8,512,128]{2,1,0:T(8,128)S(1)} %copy-done.3, f32[512,512,8]{1,0,2:T(8,128)S(1)} %get-tuple-element.596, f32[512]{0:T(512)S(1)} %broadcast_bitcast_fusion.7, f32[8,512]{1,0:T(8,128)S(1)} %max.11, f32[512]{0:T(512)S(1)} %broadcast_bitcast_fusion.6, ...), kind=kOutput, calls=%fused_computation.7.clone.1 | convolution fusion | flops 552599552 | bytes 13012992 | tf_op jit(solution)/shard_map/while/body/eval_jaxpr/hqk,kd->hqd/dot_general | solution.py:79
  166.4 2.5 collective-permute-start.4
  185.0 2.5 fusion.135
  187.6 3.7 %multiply_add_fusion.6 = f32[8,512,128]{2,1,0:T(8,128)S(1)} fusion(f32[8,512,128]{2,1,0:T(8,128)S(1)} %copy-done.3, f32[512,512,8]{1,0,2:T(8,128)S(1)} %get-tuple-element.596, f32[512]{0:T(512)S(1)} %broadcast_bitcast_fusion.7, f32[8,512]{1,0:T(8,128)S(1)} %max.11, f32[512]{0:T(512)S(1)} %broadcast_bitcast_fusion.6, ...), kind=kOutput, calls=%fused_computation.7.clone.1 | convolution fusion | flops 552599552 | bytes 13012992 | tf_op jit(solution)/shard_map/while/body/eval_jaxpr/hqk,kd->hqd/dot_general | solution.py:79
  212.2 2.5 fusion.135
  214.8 3.7 %multiply_add_fusion.6 = f32[8,512,128]{2,1,0:T(8,128)S(1)} fusion(f32[8,512,128]{2,1,0:T(8,128)S(1)} %copy-done.3, f32[512,512,8]{1,0,2:T(8,128)S(1)} %get-tuple-element.596, f32[512]{0:T(512)S(1)} %broadcast_bitcast_fusion.7, f32[8,512]{1,0:T(8,128)S(1)} %max.11, f32[512]{0:T(512)S(1)} %broadcast_bitcast_fusion.6, ...), kind=kOutput, calls=%fused_computation.7.clone.1 | convolution fusion | flops 552599552 | bytes 13012992 | tf_op jit(solution)/shard_map/while/body/eval_jaxpr/hqk,kd->hqd/dot_general | solution.py:79
  239.9 2.5 fusion.135
  242.5 3.7 %multiply_add_fusion.6 = f32[8,512,128]{2,1,0:T(8,128)S(1)} fusion(f32[8,512,128]{2,1,0:T(8,128)S(1)} %copy-done.3, f32[512,512,8]{1,0,2:T(8,128)S(1)} %get-tuple-element.596, f32[512]{0:T(512)S(1)} %broadcast_bitcast_fusion.7, f32[8,512]{1,0:T(8,128)S(1)} %max.11, f32[512]{0:T(512)S(1)} %broadcast_bitcast_fusion.6, ...), kind=kOutput, calls=%fused_computation.7.clone.1 | convolution fusion | flops 552599552 | bytes 13012992 | tf_op jit(solution)/shard_map/while/body/eval_jaxpr/hqk,kd->hqd/dot_general | solution.py:79
  267.1 2.5 fusion.135
  269.7 3.7 %multiply_add_fusion.6 = f32[8,512,128]{2,1,0:T(8,128)S(1)} fusion(f32[8,512,128]{2,1,0:T(8,128)S(1)} %copy-done.3, f32[512,512,8]{1,0,2:T(8,128)S(1)} %get-tuple-element.596, f32[512]{0:T(512)S(1)} %broadcast_bitcast_fusion.7, f32[8,512]{1,0:T(8,128)S(1)} %max.11, f32[512]{0:T(512)S(1)} %broadcast_bitcast_fusion.6, ...), kind=kOutput, calls=%fused_computation.7.clone.1 | convolution fusion | flops 552599552 | bytes 13012992 | tf_op jit(solution)/shard_map/while/body/eval_jaxpr/hqk,kd->hqd/dot_general | solution.py:79
  274.8 3.9 %select_convert_fusion = bf16[128,8,512]{2,0,1:T(8,128)(2,1)S(1)} fusion(f32[8,512,128]{2,1,0:T(8,128)} %get-tuple-element.338, f32[8,512]{1,0:T(8,128)S(1)} %get-tuple-element.339, pred[512]{0:T(512)(128)(4,1)S(1)} %broadcast_compare_fusion.1), kind=kOutput, calls=%fused_computation.34 | convolution fusion | flops 807469056 | bytes 3162624 | tf_op jit(solution)/shard_map/hqd,de->qhe/dot_general | solution.py:176
  (314 shorter events, 159.8 us)
Async XLA Ops:
  7.2 274.5 %all-gather.3.cloned.1.call-start = ((), (), s32[]{:S(2)}) async-start(), calls=%async_computation | async-start | bytes 1114112 | tf_op jit(solution)/shard_map/all_gather | solution.py:192
  12.0 272.3 %all-gather.5.cloned.1.call-start = ((), (), s32[]{:S(2)}) async-start(), calls=%async_computation.1 | async-start | bytes 1114112 | tf_op jit(solution)/shard_map/all_gather | solution.py:193
  77.3 12.0 %collective-permute-start = (bf16[2]{0:T(256)(128)(2,1)S(1)}, bf16[2]{0:T(256)(128)(2,1)S(1)}, u32[]{:S(2)}, u32[]{:S(2)}) collective-permute-start(bf16[2]{0:T(256)(128)(2,1)S(1)} %dynamic_slice.92), channel_id=1, source_target_pairs={{0,16},{16,32},{32,48},{48,64},{64,80},{80,96},{96,112},{1,17},{17... | collective-permute-start | bytes 20 | tf_op jit(solution)/shard_map/while/body/eval_jaxpr/ppermute | solution.py:15
  78.7 10.8 %collective-permute-start.4 = (bf16[2]{0:T(256)(128)(2,1)S(1)}, bf16[2]{0:T(256)(128)(2,1)S(1)}, u32[]{:S(2)}, u32[]{:S(2)}) collective-permute-start(bf16[2]{0:T(256)(128)(2,1)S(1)} %dynamic_slice.93), channel_id=1, source_target_pairs={{0,16},{16,32},{32,48},{48,64},{64,80},{80,96},{96,112},{1,17},{17... | collective-permute-start | bytes 20 | tf_op jit(solution)/shard_map/while/body/eval_jaxpr/ppermute | solution.py:15
  82.8 10.4 %collective-permute-start.2 = (bf16[256,128]{1,0:T(8,128)(2,1)S(1)}, bf16[256,128]{1,0:T(8,128)(2,1)S(1)}, u32[]{:S(2)}, u32[]{:S(2)}) collective-permute-start(bf16[256,128]{1,0:T(8,128)(2,1)S(1)} %constant_dynamic-slice_fusion.4), channel_id=1, source_target_pairs={{0,16},{16,32},{32,48},{48,64},{64,80},{80,96},{96,112},{1,17},{17... | collective-permute-start | bytes 196616 | tf_op jit(solution)/shard_map/while/body/eval_jaxpr/ppermute | solution.py:15
  84.8 10.4 %collective-permute-start.6 = (bf16[256,128]{1,0:T(8,128)(2,1)S(1)}, bf16[256,128]{1,0:T(8,128)(2,1)S(1)}, u32[]{:S(2)}, u32[]{:S(2)}) collective-permute-start(bf16[256,128]{1,0:T(8,128)(2,1)S(1)} %constant_dynamic-slice_fusion.5), channel_id=1, source_target_pairs={{0,16},{16,32},{32,48},{48,64},{64,80},{80,96},{96,112},{1,17},{17... | collective-permute-start | bytes 196616 | tf_op jit(solution)/shard_map/while/body/eval_jaxpr/ppermute | solution.py:15
  108.2 10.8 %collective-permute-start = (bf16[2]{0:T(256)(128)(2,1)S(1)}, bf16[2]{0:T(256)(128)(2,1)S(1)}, u32[]{:S(2)}, u32[]{:S(2)}) collective-permute-start(bf16[2]{0:T(256)(128)(2,1)S(1)} %dynamic_slice.92), channel_id=1, source_target_pairs={{0,16},{16,32},{32,48},{48,64},{64,80},{80,96},{96,112},{1,17},{17... | collective-permute-start | bytes 20 | tf_op jit(solution)/shard_map/while/body/eval_jaxpr/ppermute | solution.py:15
  109.5 10.7 %collective-permute-start.4 = (bf16[2]{0:T(256)(128)(2,1)S(1)}, bf16[2]{0:T(256)(128)(2,1)S(1)}, u32[]{:S(2)}, u32[]{:S(2)}) collective-permute-start(bf16[2]{0:T(256)(128)(2,1)S(1)} %dynamic_slice.93), channel_id=1, source_target_pairs={{0,16},{16,32},{32,48},{48,64},{64,80},{80,96},{96,112},{1,17},{17... | collective-permute-start | bytes 20 | tf_op jit(solution)/shard_map/while/body/eval_jaxpr/ppermute | solution.py:15
  113.6 10.3 %collective-permute-start.2 = (bf16[256,128]{1,0:T(8,128)(2,1)S(1)}, bf16[256,128]{1,0:T(8,128)(2,1)S(1)}, u32[]{:S(2)}, u32[]{:S(2)}) collective-permute-start(bf16[256,128]{1,0:T(8,128)(2,1)S(1)} %constant_dynamic-slice_fusion.4), channel_id=1, source_target_pairs={{0,16},{16,32},{32,48},{48,64},{64,80},{80,96},{96,112},{1,17},{17... | collective-permute-start | bytes 196616 | tf_op jit(solution)/shard_map/while/body/eval_jaxpr/ppermute | solution.py:15
  115.5 9.2 %collective-permute-start.6 = (bf16[256,128]{1,0:T(8,128)(2,1)S(1)}, bf16[256,128]{1,0:T(8,128)(2,1)S(1)}, u32[]{:S(2)}, u32[]{:S(2)}) collective-permute-start(bf16[256,128]{1,0:T(8,128)(2,1)S(1)} %constant_dynamic-slice_fusion.5), channel_id=1, source_target_pairs={{0,16},{16,32},{32,48},{48,64},{64,80},{80,96},{96,112},{1,17},{17... | collective-permute-start | bytes 196616 | tf_op jit(solution)/shard_map/while/body/eval_jaxpr/ppermute | solution.py:15
  137.8 8.8 %collective-permute-start = (bf16[2]{0:T(256)(128)(2,1)S(1)}, bf16[2]{0:T(256)(128)(2,1)S(1)}, u32[]{:S(2)}, u32[]{:S(2)}) collective-permute-start(bf16[2]{0:T(256)(128)(2,1)S(1)} %dynamic_slice.92), channel_id=1, source_target_pairs={{0,16},{16,32},{32,48},{48,64},{64,80},{80,96},{96,112},{1,17},{17... | collective-permute-start | bytes 20 | tf_op jit(solution)/shard_map/while/body/eval_jaxpr/ppermute | solution.py:15
  141.8 9.4 %collective-permute-start.2 = (bf16[256,128]{1,0:T(8,128)(2,1)S(1)}, bf16[256,128]{1,0:T(8,128)(2,1)S(1)}, u32[]{:S(2)}, u32[]{:S(2)}) collective-permute-start(bf16[256,128]{1,0:T(8,128)(2,1)S(1)} %constant_dynamic-slice_fusion.4), channel_id=1, source_target_pairs={{0,16},{16,32},{32,48},{48,64},{64,80},{80,96},{96,112},{1,17},{17... | collective-permute-start | bytes 196616 | tf_op jit(solution)/shard_map/while/body/eval_jaxpr/ppermute | solution.py:15
  143.7 8.7 %collective-permute-start.6 = (bf16[256,128]{1,0:T(8,128)(2,1)S(1)}, bf16[256,128]{1,0:T(8,128)(2,1)S(1)}, u32[]{:S(2)}, u32[]{:S(2)}) collective-permute-start(bf16[256,128]{1,0:T(8,128)(2,1)S(1)} %constant_dynamic-slice_fusion.5), channel_id=1, source_target_pairs={{0,16},{16,32},{32,48},{48,64},{64,80},{80,96},{96,112},{1,17},{17... | collective-permute-start | bytes 196616 | tf_op jit(solution)/shard_map/while/body/eval_jaxpr/ppermute | solution.py:15
  165.1 8.8 %collective-permute-start = (bf16[2]{0:T(256)(128)(2,1)S(1)}, bf16[2]{0:T(256)(128)(2,1)S(1)}, u32[]{:S(2)}, u32[]{:S(2)}) collective-permute-start(bf16[2]{0:T(256)(128)(2,1)S(1)} %dynamic_slice.92), channel_id=1, source_target_pairs={{0,16},{16,32},{32,48},{48,64},{64,80},{80,96},{96,112},{1,17},{17... | collective-permute-start | bytes 20 | tf_op jit(solution)/shard_map/while/body/eval_jaxpr/ppermute | solution.py:15
  166.4 8.7 %collective-permute-start.4 = (bf16[2]{0:T(256)(128)(2,1)S(1)}, bf16[2]{0:T(256)(128)(2,1)S(1)}, u32[]{:S(2)}, u32[]{:S(2)}) collective-permute-start(bf16[2]{0:T(256)(128)(2,1)S(1)} %dynamic_slice.93), channel_id=1, source_target_pairs={{0,16},{16,32},{32,48},{48,64},{64,80},{80,96},{96,112},{1,17},{17... | collective-permute-start | bytes 20 | tf_op jit(solution)/shard_map/while/body/eval_jaxpr/ppermute | solution.py:15
  169.0 9.8 %collective-permute-start.2 = (bf16[256,128]{1,0:T(8,128)(2,1)S(1)}, bf16[256,128]{1,0:T(8,128)(2,1)S(1)}, u32[]{:S(2)}, u32[]{:S(2)}) collective-permute-start(bf16[256,128]{1,0:T(8,128)(2,1)S(1)} %constant_dynamic-slice_fusion.4), channel_id=1, source_target_pairs={{0,16},{16,32},{32,48},{48,64},{64,80},{80,96},{96,112},{1,17},{17... | collective-permute-start | bytes 196616 | tf_op jit(solution)/shard_map/while/body/eval_jaxpr/ppermute | solution.py:15
  192.8 8.8 %collective-permute-start = (bf16[2]{0:T(256)(128)(2,1)S(1)}, bf16[2]{0:T(256)(128)(2,1)S(1)}, u32[]{:S(2)}, u32[]{:S(2)}) collective-permute-start(bf16[2]{0:T(256)(128)(2,1)S(1)} %dynamic_slice.92), channel_id=1, source_target_pairs={{0,16},{16,32},{32,48},{48,64},{64,80},{80,96},{96,112},{1,17},{17... | collective-permute-start | bytes 20 | tf_op jit(solution)/shard_map/while/body/eval_jaxpr/ppermute | solution.py:15
  196.7 9.4 %collective-permute-start.2 = (bf16[256,128]{1,0:T(8,128)(2,1)S(1)}, bf16[256,128]{1,0:T(8,128)(2,1)S(1)}, u32[]{:S(2)}, u32[]{:S(2)}) collective-permute-start(bf16[256,128]{1,0:T(8,128)(2,1)S(1)} %constant_dynamic-slice_fusion.4), channel_id=1, source_target_pairs={{0,16},{16,32},{32,48},{48,64},{64,80},{80,96},{96,112},{1,17},{17... | collective-permute-start | bytes 196616 | tf_op jit(solution)/shard_map/while/body/eval_jaxpr/ppermute | solution.py:15
  220.0 8.8 %collective-permute-start = (bf16[2]{0:T(256)(128)(2,1)S(1)}, bf16[2]{0:T(256)(128)(2,1)S(1)}, u32[]{:S(2)}, u32[]{:S(2)}) collective-permute-start(bf16[2]{0:T(256)(128)(2,1)S(1)} %dynamic_slice.92), channel_id=1, source_target_pairs={{0,16},{16,32},{32,48},{48,64},{64,80},{80,96},{96,112},{1,17},{17... | collective-permute-start | bytes 20 | tf_op jit(solution)/shard_map/while/body/eval_jaxpr/ppermute | solution.py:15
  221.4 8.7 %collective-permute-start.4 = (bf16[2]{0:T(256)(128)(2,1)S(1)}, bf16[2]{0:T(256)(128)(2,1)S(1)}, u32[]{:S(2)}, u32[]{:S(2)}) collective-permute-start(bf16[2]{0:T(256)(128)(2,1)S(1)} %dynamic_slice.93), channel_id=1, source_target_pairs={{0,16},{16,32},{32,48},{48,64},{64,80},{80,96},{96,112},{1,17},{17... | collective-permute-start | bytes 20 | tf_op jit(solution)/shard_map/while/body/eval_jaxpr/ppermute | solution.py:15
  223.9 9.8 %collective-permute-start.2 = (bf16[256,128]{1,0:T(8,128)(2,1)S(1)}, bf16[256,128]{1,0:T(8,128)(2,1)S(1)}, u32[]{:S(2)}, u32[]{:S(2)}) collective-permute-start(bf16[256,128]{1,0:T(8,128)(2,1)S(1)} %constant_dynamic-slice_fusion.4), channel_id=1, source_target_pairs={{0,16},{16,32},{32,48},{48,64},{64,80},{80,96},{96,112},{1,17},{17... | collective-permute-start | bytes 196616 | tf_op jit(solution)/shard_map/while/body/eval_jaxpr/ppermute | solution.py:15
  225.9 8.7 %collective-permute-start.6 = (bf16[256,128]{1,0:T(8,128)(2,1)S(1)}, bf16[256,128]{1,0:T(8,128)(2,1)S(1)}, u32[]{:S(2)}, u32[]{:S(2)}) collective-permute-start(bf16[256,128]{1,0:T(8,128)(2,1)S(1)} %constant_dynamic-slice_fusion.5), channel_id=1, source_target_pairs={{0,16},{16,32},{32,48},{48,64},{64,80},{80,96},{96,112},{1,17},{17... | collective-permute-start | bytes 196616 | tf_op jit(solution)/shard_map/while/body/eval_jaxpr/ppermute | solution.py:15
  247.7 8.8 %collective-permute-start = (bf16[2]{0:T(256)(128)(2,1)S(1)}, bf16[2]{0:T(256)(128)(2,1)S(1)}, u32[]{:S(2)}, u32[]{:S(2)}) collective-permute-start(bf16[2]{0:T(256)(128)(2,1)S(1)} %dynamic_slice.92), channel_id=1, source_target_pairs={{0,16},{16,32},{32,48},{48,64},{64,80},{80,96},{96,112},{1,17},{17... | collective-permute-start | bytes 20 | tf_op jit(solution)/shard_map/while/body/eval_jaxpr/ppermute | solution.py:15
  251.6 9.4 %collective-permute-start.2 = (bf16[256,128]{1,0:T(8,128)(2,1)S(1)}, bf16[256,128]{1,0:T(8,128)(2,1)S(1)}, u32[]{:S(2)}, u32[]{:S(2)}) collective-permute-start(bf16[256,128]{1,0:T(8,128)(2,1)S(1)} %constant_dynamic-slice_fusion.4), channel_id=1, source_target_pairs={{0,16},{16,32},{32,48},{48,64},{64,80},{80,96},{96,112},{1,17},{17... | collective-permute-start | bytes 196616 | tf_op jit(solution)/shard_map/while/body/eval_jaxpr/ppermute | solution.py:15
  (52 other events, 253.7 us)
Sparse Core Ops, SparseCore 0:
  12.1 45.3 all-gather.2
  59.6 42.9 all-gather.4
where the time goes:
time: 295 us; the launch traced here: 294 us
  starting transfers between devices  88 us (30%)
  matrix products  59.9 us (20%)
  blocking collectives  42.2 us (14%)
  other arithmetic  33.3 us (11%)
  waiting for transfers between devices  32.1 us (11%)
  local copies, waits for them, and re-layouts  21.4 us (7%)
  between operations  15.5 us (5%)
    ppermute x28, starting transfers between devices, passed_along(): lax.ppermute(value, axis, [(source, source + steps) for source in range(i...  58.9 us
    unnamed x1, blocking collectives  42.2 us
    dot_general x8, matrix products, attend(): jnp.einsum('hqk,kd->hqd', weights, value_pages, preferred_element_type=jn...  32.5 us
    ppermute x28, waiting for transfers between devices, partner(): lax.ppermute(x, axis, [(i, i ^ 1 << distance) for i in range(lax.axis_siz...  32 us
    ppermute x28, starting transfers between devices, partner(): lax.ppermute(x, axis, [(i, i ^ 1 << distance) for i in range(lax.axis_siz...  29.1 us
    reduce_sum x8, other arithmetic, attend(): denominator = denominator * factor + jnp.sum(exp_scores, axis=2)  20.3 us
    dot_general x8, matrix products, attend(): jnp.einsum('qhd,kd->hqk', rotated_queries, key_pages, preferred_element_t...  14.5 us
    while x35, local copies, waits for them, and re-layouts  9.75 us
  transfers between devices with their start and end apart: 58, of which 20 were waited for; matrix products, arithmetic and copies ran while one was open for 32% of the time, Pallas kernels for 0%

commit v1 on v0

v1 whole, which is shorter than its diff:
```python
import math

import jax
import jax.numpy as jnp
from jax import lax
from jax.experimental import pallas as pl
from jax.experimental.pallas import tpu as pltpu
from jax.sharding import PartitionSpec as P

HD = 128
PAGE = 128
TOK = 512
LH = 8
KVH = 8
PAGES = 4
SLOTS = 4
CHIPS = 4
MESH = pl.DeviceIdType.MESH
BF = jnp.bfloat16
F32 = jnp.float32
NEG = -1e30
LOGIT = math.log2(math.e) / math.sqrt(HD)


def dot(a, b, dims):
    return lax.dot_general(a, b, (dims, ((), ())), preferred_element_type=F32)


def qk(q, k):
    return dot(q, k, ((1,), (1,)))


def pv(p, v):
    return dot(p.astype(BF), v, ((1,), (0,)))


def wide(x, columns):
    return jnp.tile(x, (1, columns // x.shape[1]))


def signs():
    row = lax.broadcasted_iota(jnp.int32, (HD, HD), 0)
    column = lax.broadcasted_iota(jnp.int32, (HD, HD), 1)
    common = row & column
    parity = common & 1
    for bit in range(1, 7):
        parity = parity ^ ((common >> bit) & 1)
    return (1 - 2 * parity).astype(F32).astype(BF)


def kernel(
    q_hbm, pk_hbm, pv_hbm, owner_ref, layout_ref, length_ref,
    out_hbm, kc_hbm, vc_hbm, ks_ref, vs_ref,
    q_scr, pk_scr, pv_scr, kraw, kbuf, vbuf, acc, mx, out_scr, kc_scr, vc_scr,
    in_sem, out_sem, send_sem, recv_sem,
):
    c = lax.axis_index("ctx")
    head = lax.axis_index("head")
    y = c // 2
    k = c % 2
    g = head // 2
    sib = 2 * y + (1 - k)
    right = 2 * ((y + 1) % CHIPS) + k
    left = 2 * ((y + CHIPS - 1) % CHIPS) + k
    column = pl.ds(pl.multiple_of(g * HD, HD), HD)
    own_rows = pl.ds(pl.multiple_of(k * TOK, TOK), TOK)

    get_k = pltpu.make_async_copy(pk_hbm.at[:, column], kraw, in_sem.at[0])
    get_v = pltpu.make_async_copy(pv_hbm.at[:, column], vbuf.at[y, own_rows, pl.ds(0, HD)], in_sem.at[1])
    get_q = pltpu.make_async_copy(q_hbm, q_scr, in_sem.at[2])
    get_pk = pltpu.make_async_copy(pk_hbm, pk_scr, in_sem.at[3])
    get_pv = pltpu.make_async_copy(pv_hbm, pv_scr, in_sem.at[4])
    for copy in (get_k, get_v, get_q, get_pk, get_pv):
        copy.start()

    barrier = pltpu.get_barrier_semaphore()
    for other in (sib, left, right):
        pl.semaphore_signal(barrier, inc=1, device_id={"ctx": other}, device_id_type=MESH)

    get_k.wait()
    kbuf[y, own_rows, :] = (kraw[...].astype(F32) * LOGIT).astype(BF)
    get_v.wait()
    pl.semaphore_wait(barrier, 3)

    def block_refs(block):
        chip = block // 2
        rows = pl.ds(pl.multiple_of((block % 2) * TOK, TOK), TOK)
        return kbuf.at[chip, rows, :], vbuf.at[chip, rows, pl.ds(0, HD)]

    def copies(block, other, place):
        return [
            pltpu.make_async_remote_copy(
                src_ref=ref, dst_ref=ref, send_sem=send_sem.at[i, place], recv_sem=recv_sem.at[i, block],
                device_id={"ctx": other}, device_id_type=MESH,
            )
            for i, ref in enumerate(block_refs(block))
        ]

    def send(block, other, place):
        for copy in copies(block, other, place):
            copy.start()

    def sent(block, other, place):
        for copy in copies(block, other, place):
            copy.wait_send()

    def arrived(block):
        for copy in copies(block, sib, 0):
            copy.wait_recv()

    @pl.when(y < 3)
    def _():
        send(c, right, 0)

    @pl.when(y == 0)
    def _():
        send(c, left, 1)

    @pl.when(k == 0)
    def _():
        send(c, sib, 2)

    vbuf[:, :, HD:] = jnp.ones((CHIPS, 2 * TOK, HD), BF)

    length = length_ref[0]
    rotation = signs()
    found = jnp.int32(0)
    entry = [jnp.int32(-1)] * SLOTS
    for r in range(KVH):
        kv = layout_ref[r]
        for i in range(PAGES):
            owner = jnp.int32(0)
            for other in range(KVH):
                owner = jnp.where(kv == other, owner_ref[i * KVH + other], owner)
            mine = owner == head
            for s in range(SLOTS):
                entry[s] = jnp.where(mine & (found == s), i * KVH + kv, entry[s])
            found = found + jnp.where(mine, 1, 0)
    get_pk.wait()
    get_pv.wait()
    lanes = lax.broadcasted_iota(jnp.int32, (1, SLOTS), 1)
    page_row = lax.broadcasted_iota(jnp.int32, (PAGE, HD), 0)
    for source, cache, scale_ref in ((pk_scr, kc_scr, ks_ref), (pv_scr, vc_scr, vs_ref)):
        scale_row = jnp.zeros((1, SLOTS), F32)
        for s in range(SLOTS):
            raw = jnp.zeros((PAGE, HD), BF)
            for e in range(PAGES * KVH):
                page, kv = divmod(e, KVH)
                here = jnp.full((PAGE, HD), entry[s], jnp.int32) == e
                raw = jnp.where(here, source[page * PAGE : (page + 1) * PAGE, kv * HD : (kv + 1) * HD], raw)
            live = page_row + (c * TOK + (entry[s] >> 3) * PAGE) < length
            kept = jnp.where(live, raw.astype(F32), 0.0).astype(BF)
            rotated = dot(kept, rotation, ((1,), (0,))) * (1.0 / math.sqrt(HD))
            largest = jnp.max(jnp.max(jnp.abs(rotated), axis=1, keepdims=True), axis=0, keepdims=True)
            scale = (largest / 448.0 + 1e-6).astype(BF).astype(F32)
            stored = (rotated / scale).astype(BF).astype(F32)
            there = (jnp.zeros((1, 1), jnp.int32) + found) > s
            cache[s] = jnp.where(there, stored, 0.0).astype(BF)
            scale_row = jnp.where((lanes == s) & there, scale, scale_row)
        scale_ref[...] = scale_row.astype(BF)
    put_kc = pltpu.make_async_copy(kc_scr, kc_hbm.at[0], out_sem.at[0])
    put_vc = pltpu.make_async_copy(vc_scr, vc_hbm.at[0], out_sem.at[1])
    put_kc.start()
    put_vc.start()

    get_q.wait()

    def heads_q(h, rows=slice(None)):
        return q_scr[rows, h * HD : (h + 1) * HD]

    half = TOK // 2
    mask = lax.broadcasted_iota(jnp.int32, (half, half), 1) <= lax.broadcasted_iota(jnp.int32, (half, half), 0)
    k_own = kbuf[y, own_rows, :]
    v_own = vbuf[y, own_rows, :]
    for h in range(LH):
        for part in range(2):
            rows = slice(part * half, (part + 1) * half)
            s = qk(heads_q(h, rows), k_own[: (part + 1) * half])
            last = jnp.where(mask, s[:, part * half :], NEG)
            s = last if part == 0 else jnp.concatenate([s[:, :half], last], axis=1)
            m = jnp.broadcast_to(jnp.max(s, axis=1, keepdims=True), (half, HD))
            mx[h, rows, :] = m
            acc[h, rows, :] = pv(jnp.exp2(s - wide(m, s.shape[1])), v_own[: (part + 1) * half])

    def full(kb, vb):
        for h in range(LH):
            s = qk(heads_q(h), kb)
            old = mx[h]
            new = jnp.maximum(old, jnp.max(s, axis=1, keepdims=True))
            factor = jnp.exp2(old - new)
            mx[h] = new
            acc[h] = acc[h] * wide(factor, 2 * HD) + pv(jnp.exp2(s - wide(new, s.shape[1])), vb)

    @pl.when(k == 1)
    def _():
        arrived(sib)
        other_rows = pl.ds(0, TOK)
        full(kbuf[y, other_rows, :], vbuf[y, other_rows, :])

    def chip_of(t):
        return jnp.where(t == 0, y - 1, t - 1)

    def relays(t):
        return (t == 0) & ((y == 1) | (y == 2))

    def handle(t):
        block = 2 * chip_of(t) + k
        arrived(block)
        send(block, sib, 3 + t)

        @pl.when(relays(t))
        def _():
            send(block, right, 6)

    @pl.when(y > 0)
    def _():
        handle(0)

    def step(t, carry):
        @pl.when(t + 1 < y)
        def _():
            handle(t + 1)

        chip = chip_of(t)
        arrived(2 * chip + (1 - k))
        full(kbuf[chip], vbuf[chip])
        return carry

    lax.fori_loop(0, y, step, 0)

    row = lax.broadcasted_iota(jnp.int32, (TOK, HD), 0) + c * TOK
    for h in range(LH):
        o = acc[h, :, :HD] / acc[h, :, HD:]
        out_scr[:, h * HD : (h + 1) * HD] = jnp.where(row < length, o, 0.0).astype(BF)
    put_o = pltpu.make_async_copy(out_scr, out_hbm, out_sem.at[2])
    put_o.start()

    @pl.when(y < 3)
    def _():
        sent(c, right, 0)

    @pl.when(y == 0)
    def _():
        sent(c, left, 1)

    @pl.when(k == 0)
    def _():
        sent(c, sib, 2)

    def finish(t, carry):
        sent(2 * chip_of(t) + k, sib, 3 + t)

        @pl.when(relays(t))
        def _():
            sent(2 * chip_of(t) + k, right, 6)

        return carry

    lax.fori_loop(0, y, finish, 0)
    put_kc.wait()
    put_vc.wait()
    put_o.wait()


def per_device(queries, prompt_keys, prompt_values, owner_map, head_layout, prompt_length):
    any_ = pl.BlockSpec(memory_space=pl.ANY)
    smem = pl.BlockSpec(memory_space=pltpu.SMEM)
    vmem = pl.BlockSpec(memory_space=pltpu.VMEM)
    return pl.pallas_call(
        kernel,
        out_shape=(
            jax.ShapeDtypeStruct((TOK, LH * HD), BF),
            jax.ShapeDtypeStruct((1, SLOTS, PAGE, HD), BF),
            jax.ShapeDtypeStruct((1, SLOTS, PAGE, HD), BF),
            jax.ShapeDtypeStruct((1, SLOTS), BF),
            jax.ShapeDtypeStruct((1, SLOTS), BF),
        ),
        in_specs=[any_, any_, any_, smem, smem, smem],
        out_specs=(any_, any_, any_, vmem, vmem),
        scratch_shapes=[
            pltpu.VMEM((TOK, LH * HD), BF),
            pltpu.VMEM((TOK, KVH * HD), BF),
            pltpu.VMEM((TOK, KVH * HD), BF),
            pltpu.VMEM((TOK, HD), BF),
            pltpu.VMEM((CHIPS, 2 * TOK, HD), BF),
            pltpu.VMEM((CHIPS, 2 * TOK, 2 * HD), BF),
            pltpu.VMEM((LH, TOK, 2 * HD), F32),
            pltpu.VMEM((LH, TOK, HD), F32),
            pltpu.VMEM((TOK, LH * HD), BF),
            pltpu.VMEM((SLOTS, PAGE, HD), BF),
            pltpu.VMEM((SLOTS, PAGE, HD), BF),
            pltpu.SemaphoreType.DMA((5,)),
            pltpu.SemaphoreType.DMA((3,)),
            pltpu.SemaphoreType.DMA((2, 7)),
            pltpu.SemaphoreType.DMA((2, 8)),
        ],
        compiler_params=pltpu.CompilerParams(
            collective_id=0, has_side_effects=True, vmem_limit_bytes=56 << 20
        ),
        name="prefill",
    )(queries, prompt_keys, prompt_values, owner_map.reshape(-1), head_layout, prompt_length)


def solution(mesh):
    in_specs = (P("ctx", "head"), P("ctx", None), P("ctx", None), P("ctx", None, None), P(), P())
    out_specs = (
        P("ctx", "head"),
        P("ctx", "head", None, None),
        P("ctx", "head", None, None),
        P("ctx", "head"),
        P("ctx", "head"),
    )
    return jax.shard_map(
        per_device, mesh=mesh, in_specs=in_specs, out_specs=out_specs, check_vma=False
    )
```

time: 295 us -> 38.1 us (0.13)
  the two profiles are of different devices: /device:TPU:0 before, /device:TPU:118 now
where the time goes in v1:
time: 38.1 us; the launch traced here: 37.9 us
  Pallas kernels  29.7 us (78%)
  local copies, waits for them, and re-layouts  6.2 us (16%)
  between operations  1.32 us (3%)
  other arithmetic  0.66 us (2%)
    pallas_call x1, Pallas kernels, per_device(): pl.pallas_call(kernel, out_shape=(jax.ShapeDtypeStruct((TOK, LH * HD), BF...  29.7 us
    unnamed x16, local copies, waits for them, and re-layouts  5.61 us

profile of v1, /device:TPU:118, one launch (start us, length us, event | category | flops | bytes accessed | tf_op | source)
XLA Modules:
  0.0 37.9 jit_solution(743654727128368104)
XLA Ops:
  0.6 0.0 copy-start.2
  1.3 0.5 %broadcast.3 = s32[]{:T(128)} broadcast(s32[]{:T(128)} %constant.4), dimensions={} | broadcast | bytes 8 | tf_op args[3]
  1.8 0.0 copy-done.2
  1.8 0.7 %reduce.3 = s32[4,8]{1,0:T(4,128)S(1)} reduce(s32[4,8,1]{1,2,0:T(1,128)S(1)} %copy-done.2, s32[]{:T(128)} %broadcast.3), dimensions={2}, to_apply=%param.9.reduce_sub_computation.3 | reduce | bytes 260 | tf_op args[3]
  2.5 0.6 %reshape.13.owner_ref = s32[32]{0:T(128)} reshape(s32[4,8]{1,0:T(4,128)S(1)} %reduce.3) | data formatting | bytes 256 | tf_op jit(solution)/shard_map/reshape | solution.py:301
  3.1 29.7 %prefill.1 = (bf16[512,1024]{1,0:T(8,128)(2,1)}, bf16[1,4,128,128]{3,2,1,0:T(8,128)(2,1)}, bf16[1,4,128,128]{3,2,1,0:T(8,128)(2,1)}, bf16[1,4]{1,0:T(2,128)(2,1)}, bf16[1,4]{1,0:T(2,128)(2,1)}) custom-call(bf16[512,1024]{1,0:T(8,128)(2,1)} %q_hbm.1, bf16[512,1024]{1,0:T(8,128)(2,1)} %pk_hbm.1, bf16[512,1024]{1,0:T(8,128)(2,1)} %pv_hbm.1, ...), custom_call_target="tpu_custom_call" | custom-call | tf_op jit(solution)/shard_map/prefill/pallas_call | solution.py:269
  32.8 0.0 copy-start.1
  32.8 2.3 %copy.17 = bf16[512,1024]{1,0:T(8,128)(2,1)} copy(bf16[512,1024]{1,0:T(8,128)(2,1)} %get-tuple-element.10) | data formatting | bytes 2097152
  35.1 0.0 copy-done.1
  35.1 0.0 copy-start
  35.1 0.7 %copy.18 = bf16[1,4,128,128]{3,2,1,0:T(8,128)(2,1)} copy(bf16[1,4,128,128]{3,2,1,0:T(8,128)(2,1)S(1)} %copy-done.1) | data formatting | bytes 262144
  35.7 0.3 copy-done
  36.0 0.0 copy-start.4
  36.0 0.7 %copy.19 = bf16[1,4,128,128]{3,2,1,0:T(8,128)(2,1)} copy(bf16[1,4,128,128]{3,2,1,0:T(8,128)(2,1)S(1)} %copy-done) | data formatting | bytes 262144
  36.7 0.0 copy-done.4
  36.7 0.0 copy-start.3
  36.7 0.5 %copy.20 = bf16[1,4]{1,0:T(2,128)(2,1)} copy(bf16[1,4]{1,0:T(2,128)(2,1)S(1)} %copy-done.4) | data formatting | bytes 16
  37.2 0.2 copy-done.3
  37.4 0.5 %copy.21 = bf16[1,4]{1,0:T(2,128)(2,1)} copy(bf16[1,4]{1,0:T(2,128)(2,1)S(1)} %copy-done.3) | data formatting | bytes 16
Async XLA Ops:
  0.6 1.2 %copy-start.2 = (s32[4,8,1]{1,2,0:T(1,128)S(1)}, s32[4,8,1]{1,2,0:T(1,128)}, u32[]{:S(2)}) copy-start(s32[4,8,1]{1,2,0:T(1,128)} %param.9) | copy-start | bytes 388
  32.8 2.3 %copy-start.1 = (bf16[1,4,128,128]{3,2,1,0:T(8,128)(2,1)S(1)}, bf16[1,4,128,128]{3,2,1,0:T(8,128)(2,1)}, u32[]{:S(2)}) copy-start(bf16[1,4,128,128]{3,2,1,0:T(8,128)(2,1)} %get-tuple-element.11) | copy-start | bytes 393220
  35.1 1.0 %copy-start = (bf16[1,4,128,128]{3,2,1,0:T(8,128)(2,1)S(1)}, bf16[1,4,128,128]{3,2,1,0:T(8,128)(2,1)}, u32[]{:S(2)}) copy-start(bf16[1,4,128,128]{3,2,1,0:T(8,128)(2,1)} %get-tuple-element.12) | copy-start | bytes 393220
  36.0 0.7 %copy-start.4 = (bf16[1,4]{1,0:T(2,128)(2,1)S(1)}, bf16[1,4]{1,0:T(2,128)(2,1)}, u32[]{:S(2)}) copy-start(bf16[1,4]{1,0:T(2,128)(2,1)} %get-tuple-element.13) | copy-start | bytes 28
  36.7 0.7 %copy-start.3 = (bf16[1,4]{1,0:T(2,128)(2,1)S(1)}, bf16[1,4]{1,0:T(2,128)(2,1)}, u32[]{:S(2)}) copy-start(bf16[1,4]{1,0:T(2,128)(2,1)} %get-tuple-element.14) | copy-start | bytes 28

commit v2 on v1

v2 whole, which is shorter than its diff:
```python
import math

import jax
import jax.numpy as jnp
from jax import lax
from jax.experimental import pallas as pl
from jax.experimental.pallas import tpu as pltpu
from jax.sharding import PartitionSpec as P

HD = 128
PAGE = 128
TOK = 512
LH = 8
KVH = 8
PAGES = 4
SLOTS = 4
CHIPS = 4
MESH = pl.DeviceIdType.MESH
HALF = TOK // 2
GIVEN = 0
BF = jnp.bfloat16
F32 = jnp.float32
NEG = -1e30
LOGIT = math.log2(math.e) / math.sqrt(HD)


def dot(a, b, dims):
    return lax.dot_general(a, b, (dims, ((), ())), preferred_element_type=F32)


def qk(q, k):
    return dot(q, k, ((1,), (1,)))


def pv(p, v):
    return dot(p.astype(BF), v, ((1,), (0,)))


def wide(x, columns):
    return jnp.tile(x, (1, columns // x.shape[1]))


def signs():
    row = lax.broadcasted_iota(jnp.int32, (HD, HD), 0)
    column = lax.broadcasted_iota(jnp.int32, (HD, HD), 1)
    common = row & column
    parity = common & 1
    for bit in range(1, 7):
        parity = parity ^ ((common >> bit) & 1)
    return (1 - 2 * parity).astype(F32).astype(BF)


def kernel(
    q_hbm, pk_hbm, pv_hbm, length_ref, out_ref,
    q_scr, store, acc, mx, fq, facc, fmx, fout,
    in_sem, own_sem, y_send, y_recv, s_send, s_recv, q_send, q_recv, o_send, o_recv,
):
    c = lax.axis_index("ctx")
    head = lax.axis_index("head")
    y = c // 2
    k = c % 2
    g = head // 2
    sib = {"ctx": 2 * y + (1 - k)}
    right = {"ctx": 2 * ((y + 1) % CHIPS) + k}
    left = {"ctx": 2 * ((y + CHIPS - 1) % CHIPS) + k}
    other_end = {"ctx": 7 - c}
    column = pl.ds(pl.multiple_of(g * HD, HD), HD)
    home = y == 3
    helper = y == 0
    inputs = (pk_hbm, pv_hbm)

    barrier = pltpu.get_barrier_semaphore()
    others = (sib, left, right, other_end) if GIVEN else (sib, left, right)
    for other in others:
        pl.semaphore_signal(barrier, inc=1, device_id=other, device_id_type=MESH)

    def piece(chip, parity, kind, a):
        return store.at[chip, kind, a, pl.ds(pl.multiple_of(parity * HALF, HALF), HALF), :]

    def raw(kind, a):
        return inputs[kind].at[pl.ds(a * HALF, HALF), column]

    def both(a):
        return ((0, a), (1, a))

    get_own = [
        pltpu.make_async_copy(raw(kind, a), piece(y, k, kind, a), own_sem.at[kind, a]) for a in range(2) for kind in range(2)
    ]
    get_q = pltpu.make_async_copy(q_hbm, q_scr, in_sem)
    for copy in (*get_own, get_q):
        copy.start()

    def remote(src, dst, send_sem, recv_sem, device):
        return pltpu.make_async_remote_copy(
            src_ref=src, dst_ref=dst, send_sem=send_sem, recv_sem=recv_sem, device_id=device, device_id_type=MESH
        )

    def own_over_y(a, device, place, act):
        for kind in range(2):
            act(remote(raw(kind, a), piece(y, k, kind, a), y_send.at[place, kind, a], y_recv.at[y, kind, a], device))

    def over_y(chip, a, device, place, act):
        for kind in range(2):
            ref = piece(chip, k, kind, a)
            act(remote(ref, ref, y_send.at[place, kind, a], y_recv.at[chip, kind, a], device))

    def own_over_core(act):
        for a in range(2):
            for kind in range(2):
                act(remote(raw(kind, a), piece(y, k, kind, a), s_send.at[y, kind, a], s_recv.at[y, kind, a], sib))

    def over_core(chip, parity, a, act):
        for kind in range(2):
            ref = piece(chip, parity, kind, a)
            act(remote(ref, ref, s_send.at[chip, kind, a], s_recv.at[chip, kind, a], sib))

    def ask(f):
        cols = pl.ds((LH - GIVEN + f) * HD, HD)
        return remote(q_hbm.at[:, cols], fq.at[f], q_send.at[f], q_recv.at[f], other_end)

    def give_back(f):
        cols = pl.ds((LH - GIVEN + f) * HD, HD)
        return remote(fout.at[f], out_ref.at[:, cols], o_send.at[f], o_recv.at[f], other_end)

    def start(copy):
        copy.start()

    def wait_recv(copy):
        copy.wait_recv()

    def wait_send(copy):
        copy.wait_send()

    chunks = jnp.where(helper, CHIPS - 1 if GIVEN else 0, y)

    def source(i):
        return jnp.where(helper, jnp.where(i == 0, 1, jnp.where(i == 1, 3, 2)), jnp.where(i == 0, y - 1, i - 1))

    def sends(a, act):
        @pl.when(y < (4 if GIVEN else 3))
        def _():
            own_over_y(a, right, 0, act)

        @pl.when(y < (3 if GIVEN else 1))
        def _():
            own_over_y(a, left, 1, act)

    def asks(act):
        if GIVEN:
            @pl.when(home)
            def _():
                for f in range(GIVEN):
                    act(ask(f))

    def core_sends(act):
        @pl.when((k == 0) | (helper & (GIVEN > 0)))
        def _():
            own_over_core(act)

    def forwards(i, a, act):
        over_core(source(i), k, a, act)

        @pl.when((i == 0) & ((y == 1) | (y == 2)))
        def _():
            over_y(source(i), a, right, 2, act)

    def first(i, a):
        over_y(source(i), a, right, 0, wait_recv)
        forwards(i, a, start)

    def third(i, a):
        over_core(source(i), 1 - k, a, wait_recv)

    pl.semaphore_wait(barrier, len(others))
    asks(start)
    sends(0, start)
    core_sends(start)

    length = length_ref[0]
    get_q.wait()
    q_scr[...] = (q_scr[...].astype(F32) * LOGIT).astype(BF)
    for copy in get_own:
        copy.wait()

    ones = jnp.ones((2 * TOK, HD), BF)

    def with_ones(v):
        return jnp.concatenate([v, ones[: v.shape[0]]], axis=1)

    mask = lax.broadcasted_iota(jnp.int32, (HALF, HALF), 1) <= lax.broadcasted_iota(jnp.int32, (HALF, HALF), 0)

    class Own:
        def __init__(self, h):
            self.h = h

        def q(self, rows=slice(None)):
            return q_scr[rows, self.h * HD : (self.h + 1) * HD]

        def state(self):
            return mx.at[self.h], acc.at[self.h]

    class Foreign:
        def __init__(self, f):
            self.f = f

        def q(self, rows=slice(None)):
            return fq[self.f, rows, :]

        def state(self):
            return fmx, facc

    def block(chip, kind, parity):
        rows = pl.ds(pl.multiple_of(parity * HALF, HALF), HALF)
        return jnp.concatenate([store[chip, kind, a, rows, :] for a in range(2)], axis=0)

    def chunk(chip, kind):
        return store[chip, kind].reshape(2 * TOK, HD)

    def causal(items, kb, vb):
        before = kb.shape[0] - TOK
        vb = with_ones(vb)
        for item in items:
            top, total = item.state()
            for part in range(2):
                rows = slice(part * HALF, (part + 1) * HALF)
                keys = before + (part + 1) * HALF
                s = qk(item.q(rows), kb[:keys])
                last = jnp.where(mask, s[:, keys - HALF :], NEG)
                s = last if keys == HALF else jnp.concatenate([s[:, : keys - HALF], last], axis=1)
                t = jnp.broadcast_to(jnp.max(s, axis=1, keepdims=True), (HALF, HD))
                top[rows, :] = t
                total[rows, :] = pv(jnp.exp2(s - wide(t, keys)), vb[:keys])

    def full(items, kb, vb):
        vb = with_ones(vb)
        for item in items:
            top, total = item.state()
            s = qk(item.q(), kb)
            old = top[...]
            new = jnp.maximum(old, jnp.max(s, axis=1, keepdims=True))
            factor = jnp.exp2(old - new)
            top[...] = new
            total[...] = total[...] * wide(factor, 2 * HD) + pv(jnp.exp2(s - wide(new, s.shape[1])), vb)

    own = [Own(h) for h in range(LH)]
    kept_heads = own[: LH - GIVEN]

    def on_own(condition, run):
        if GIVEN:
            pl.when(condition & home)(lambda: run(kept_heads))
            pl.when(condition & jnp.logical_not(home))(lambda: run(own))
        else:
            pl.when(condition)(lambda: run(own))

    on_own(c >= 0, lambda items: causal(items, block(y, 0, k), block(y, 1, k)))
    sends(1, start)

    @pl.when((k == 1) | (helper & (GIVEN > 0)))
    def _():
        for a in range(2):
            over_core(y, 1 - k, a, wait_recv)

    on_own(k == 1, lambda items: full(items, block(y, 0, 0), block(y, 1, 0)))

    near = y - 1
    two = (y == 3) | (helper & (GIVEN > 0))

    @pl.when(chunks > 0)
    def _():
        first(0, 0)

    @pl.when(two)
    def _():
        first(1, 0)

    @pl.when(chunks > 0)
    def _():
        third(0, 0)

    on_own(y > 0, lambda items: full(items, store[near, 0, 0], store[near, 1, 0]))

    @pl.when(chunks > 0)
    def _():
        first(0, 1)

    @pl.when(two)
    def _():
        first(1, 1)
        third(1, 0)

    on_own(y == 3, lambda items: full(items, store[0, 0, 0], store[0, 1, 0]))

    @pl.when(chunks > 0)
    def _():
        third(0, 1)

    on_own(y > 0, lambda items: full(items, store[near, 0, 1], store[near, 1, 1]))

    @pl.when(two)
    def _():
        for a in range(2):
            first(2, a)
        third(1, 1)

    on_own(y == 3, lambda items: full(items, store[0, 0, 1], store[0, 1, 1]))

    @pl.when(y == 2)
    def _():
        for a in range(2):
            first(1, a)
        for a in range(2):
            third(1, a)

    @pl.when(two)
    def _():
        for a in range(2):
            third(2, a)

    last = 3 - y + jnp.where(y == 3, 1, 0) - jnp.where(y == 2, 1, 0)
    on_own((y == 2) | (y == 3), lambda items: full(items, chunk(last, 0), chunk(last, 1)))

    row = lax.broadcasted_iota(jnp.int32, (TOK, HD), 0)

    def normal(total, position):
        o = total[:, :HD] / total[:, HD:]
        return jnp.where(row + position < length, o, 0.0).astype(BF)

    if GIVEN:
        @pl.when(helper)
        def _():
            for f in range(GIVEN):
                ask(f).wait_recv()
                fq[f] = (fq[f].astype(F32) * LOGIT).astype(BF)
                item = Foreign(f)

                @pl.when(k == 0)
                def _():
                    causal(
                        [item],
                        jnp.concatenate([block(3, 0, 0), block(3, 0, 1)], axis=0),
                        jnp.concatenate([block(3, 1, 0), block(3, 1, 1)], axis=0),
                    )

                @pl.when(k == 1)
                def _():
                    causal([item], block(3, 0, 0), block(3, 1, 0))

                for chip in (0, 1, 2):
                    full([item], chunk(chip, 0), chunk(chip, 1))
                fout[f] = normal(facc, (7 - c) * TOK)
                give_back(f).start()

    def finish(items):
        for item in items:
            out_ref[:, item.h * HD : (item.h + 1) * HD] = normal(acc.at[item.h], c * TOK)

    finish(kept_heads)
    if GIVEN:
        @pl.when(jnp.logical_not(home))
        def _():
            finish(own[LH - GIVEN :])

        @pl.when(home)
        def _():
            for f in range(GIVEN):
                give_back(f).wait_recv()

    asks(wait_send)
    for a in range(2):
        sends(a, wait_send)
    core_sends(wait_send)

    def done(i, carry):
        for a in range(2):
            forwards(i, a, wait_send)
        return carry

    lax.fori_loop(0, chunks, done, 0)

    if GIVEN:
        @pl.when(y == 1)
        def _():
            for a in range(2):
                over_y(2, a, left, 3, wait_send)

        @pl.when(helper)
        def _():
            for f in range(GIVEN):
                give_back(f).wait_send()


def hand_over(
    att_ref, pk_hbm, pv_hbm, owner_ref, layout_ref, length_ref,
    att, kc, vc, ks, vs,
    raw, made, b_ks, b_vs, att_sem, in_sem, out_sem,
):
    head = lax.axis_index("head")
    start = lax.axis_index("ctx") * TOK
    put = pltpu.make_async_copy(att_ref, att, att_sem)
    put.start()

    length = length_ref[0]
    found = jnp.int32(0)
    entry = [jnp.int32(0)] * SLOTS
    for r in range(KVH):
        kv = layout_ref[r]
        for i in range(PAGES):
            mine = owner_ref[i, 0, kv] == head
            for s in range(SLOTS):
                entry[s] = jnp.where(mine & (found == s), i * KVH + kv, entry[s])
            found = found + jnp.where(mine, 1, 0)
    gets = []
    for kind, source in enumerate((pk_hbm, pv_hbm)):
        for s in range(SLOTS):
            rows = pl.ds(pl.multiple_of((entry[s] >> 3) * PAGE, PAGE), PAGE)
            columns = pl.ds(pl.multiple_of((entry[s] & 7) * HD, HD), HD)
            gets.append(pltpu.make_async_copy(source.at[rows, columns], raw.at[kind, s], in_sem.at[kind, s]))
    for copy in gets:
        copy.start()
    rotation = signs()
    lanes = lax.broadcasted_iota(jnp.int32, (1, SLOTS), 1)
    page_row = lax.broadcasted_iota(jnp.int32, (PAGE, HD), 0)
    for copy in gets:
        copy.wait()
    puts = []
    for kind, (cache, scale_out, scale_scr) in enumerate(((kc, ks, b_ks), (vc, vs, b_vs))):
        kept = []
        for s in range(SLOTS):
            live = page_row + (start + (entry[s] >> 3) * PAGE) < length
            kept.append(jnp.where(live, raw[kind, s].astype(F32), 0.0).astype(BF))
        rotated = dot(jnp.concatenate(kept, axis=0), rotation, ((1,), (0,))) * (1.0 / math.sqrt(HD))
        rotated = rotated.reshape(SLOTS, PAGE, HD)
        largest = jnp.max(jnp.max(jnp.abs(rotated), axis=1, keepdims=True), axis=2, keepdims=True)
        scales = (largest / 448.0 + 1e-6).astype(BF).astype(F32)
        stored = rotated / scales
        scale_row = jnp.zeros((1, SLOTS), F32)
        for s in range(SLOTS):
            there = (jnp.zeros((1, 1), jnp.int32) + found) > s
            made[kind, s] = jnp.where(there, stored[s], 0.0).astype(BF)
            scale_row = jnp.where((lanes == s) & there, scales[s], scale_row)
        scale_scr[...] = scale_row.astype(BF)
        puts.append(pltpu.make_async_copy(made.at[kind], cache.at[0], out_sem.at[kind, 0]))
        puts.append(pltpu.make_async_copy(scale_scr, scale_out, out_sem.at[kind, 1]))
        for copy in puts[-2:]:
            copy.start()
    put.wait()
    for copy in puts:
        copy.wait()


def per_device(queries, prompt_keys, prompt_values, owner_map, head_layout, prompt_length):
    any_ = pl.BlockSpec(memory_space=pl.ANY)
    smem = pl.BlockSpec(memory_space=pltpu.SMEM)
    vmem = pl.BlockSpec(memory_space=pltpu.VMEM)
    dma = pltpu.SemaphoreType.DMA
    given = max(GIVEN, 1)
    attention = pl.pallas_call(
        kernel,
        out_shape=pltpu.VMEM((TOK, LH * HD), BF),
        in_specs=[any_, any_, any_, smem],
        out_specs=vmem,
        scratch_shapes=[
            pltpu.VMEM((TOK, LH * HD), BF),
            pltpu.VMEM((CHIPS, 2, 2, TOK, HD), BF),
            pltpu.VMEM((LH, TOK, 2 * HD), F32),
            pltpu.VMEM((LH, TOK, HD), F32),
            pltpu.VMEM((given, TOK, HD), BF),
            pltpu.VMEM((TOK, 2 * HD), F32),
            pltpu.VMEM((TOK, HD), F32),
            pltpu.VMEM((given, TOK, HD), BF),
            dma,
            dma((2, 2)),
            dma((4, 2, 2)),
            dma((CHIPS, 2, 2)),
            dma((CHIPS, 2, 2)),
            dma((CHIPS, 2, 2)),
            dma((given,)),
            dma((given,)),
            dma((given,)),
            dma((given,)),
        ],
        compiler_params=pltpu.CompilerParams(
            collective_id=0, has_side_effects=True, vmem_limit_bytes=56 << 20
        ),
        name="prefill",
    )(queries, prompt_keys, prompt_values, prompt_length)
    return pl.pallas_call(
        hand_over,
        out_shape=(
            jax.ShapeDtypeStruct((TOK, LH * HD), BF),
            jax.ShapeDtypeStruct((1, SLOTS, PAGE, HD), BF),
            jax.ShapeDtypeStruct((1, SLOTS, PAGE, HD), BF),
            jax.ShapeDtypeStruct((1, SLOTS), BF),
            jax.ShapeDtypeStruct((1, SLOTS), BF),
        ),
        in_specs=[vmem, any_, any_, smem, smem, smem],
        out_specs=(any_,) * 5,
        scratch_shapes=[
            pltpu.VMEM((2, SLOTS, PAGE, HD), BF),
            pltpu.VMEM((2, SLOTS, PAGE, HD), BF),
            pltpu.VMEM((1, SLOTS), BF),
            pltpu.VMEM((1, SLOTS), BF),
            dma,
            dma((2, SLOTS)),
            dma((2, 2)),
        ],
        compiler_params=pltpu.CompilerParams(vmem_limit_bytes=8 << 20),
        name="hand_over",
    )(attention, prompt_keys, prompt_values, owner_map.transpose(0, 2, 1), head_layout, prompt_length)


def solution(mesh):
    in_specs = (P("ctx", "head"), P("ctx", None), P("ctx", None), P("ctx", None, None), P(), P())
    out_specs = (
        P("ctx", "head"),
        P("ctx", "head", None, None),
        P("ctx", "head", None, None),
        P("ctx", "head"),
        P("ctx", "head"),
    )
    return jax.shard_map(
        per_device, mesh=mesh, in_specs=in_specs, out_specs=out_specs, check_vma=False
    )
```

time: 38.1 us -> 30.1 us (0.79)
  the two profiles are of different devices: /device:TPU:118 before, /device:TPU:26 now
where the time goes in v2:
time: 30.1 us; the launch traced here: 29.9 us
  Pallas kernels  28.4 us (94%)
  between operations  1.51 us (5%)
    pallas_call x1, Pallas kernels, per_device(): pl.pallas_call(kernel, out_shape=pltpu.VMEM((TOK, LH * HD), BF), in_specs...  26.4 us
    pallas_call x1, Pallas kernels, per_device(): pl.pallas_call(hand_over, out_shape=(jax.ShapeDtypeStruct((TOK, LH * HD),...  2.04 us

profile of v2, /device:TPU:26, one launch (start us, length us, event | category | flops | bytes accessed | tf_op | source)
XLA Modules:
  0.0 29.9 jit_solution(15069756443630289258)
XLA Ops:
  1.3 0.0 copy-start
  1.3 0.0 copy-start.1
  1.3 0.0 copy-start.2
  1.3 0.0 copy-start.3
  1.3 26.4 %prefill.1.att_ref = bf16[512,1024]{1,0:T(8,128)(2,1)S(1)} custom-call(bf16[512,1024]{1,0:T(8,128)(2,1)} %q_hbm.1, bf16[512,1024]{1,0:T(8,128)(2,1)} %pk_hbm.3, bf16[512,1024]{1,0:T(8,128)(2,1)} %pv_hbm.3, s32[1]{0:T(128)S(6)} %copy.12.length_ref), custom_call_target="tpu_custom_call" | custom-call | tf_op jit(solution)/shard_map/prefill/pallas_call | solution.py:457
  27.7 0.0 copy-done
  27.7 0.0 copy-done.1
  27.7 0.0 copy-done.2
  27.7 0.0 copy-done.3
  27.7 2.0 %hand_over.1 = (bf16[512,1024]{1,0:T(8,128)(2,1)}, bf16[1,4,128,128]{3,2,1,0:T(8,128)(2,1)}, bf16[1,4,128,128]{3,2,1,0:T(8,128)(2,1)}, bf16[1,4]{1,0:T(2,128)(2,1)}, bf16[1,4]{1,0:T(2,128)(2,1)}) custom-call(bf16[512,1024]{1,0:T(8,128)(2,1)S(1)} %prefill.1.att_ref, bf16[512,1024]{1,0:T(8,128)(2,1)S(1)} %copy-done, bf16[512,1024]{1,0:T(8,128)(2,1)S(1)} %copy-done.1, ...), custom_call_target="tpu_custom_call" | custom-call | tf_op jit(solution)/shard_map/hand_over/pallas_call | solution.py:487
Async XLA Ops:
  1.3 26.4 %copy-start = (bf16[512,1024]{1,0:T(8,128)(2,1)S(1)}, bf16[512,1024]{1,0:T(8,128)(2,1)}, u32[]{:S(2)}) copy-start(bf16[512,1024]{1,0:T(8,128)(2,1)} %pk_hbm.3) | copy-start | bytes 3145732
  1.3 26.4 %copy-start.1 = (bf16[512,1024]{1,0:T(8,128)(2,1)S(1)}, bf16[512,1024]{1,0:T(8,128)(2,1)}, u32[]{:S(2)}) copy-start(bf16[512,1024]{1,0:T(8,128)(2,1)} %pv_hbm.3) | copy-start | bytes 3145732
  1.3 26.4 %copy-start.2 = (s32[4,8,1]{1,2,0:T(1,128)S(1)}, s32[4,8,1]{1,2,0:T(1,128)}, u32[]{:S(2)}) copy-start(s32[4,8,1]{1,2,0:T(1,128)} %param.9) | copy-start | bytes 388
  1.3 26.4 %copy-start.3 = (s32[8]{0:T(128)S(1)}, s32[8]{0:T(128)}, u32[]{:S(2)}) copy-start(s32[8]{0:T(128)} %layout_ref.1) | copy-start | bytes 100

commit v3 on v2

--- a/solution.py
+++ b/solution.py
@@ -17,7 +17,7 @@
 CHIPS = 4
 MESH = pl.DeviceIdType.MESH
 HALF = TOK // 2
-GIVEN = 0
+GIVEN = 1
 BF = jnp.bfloat16
 F32 = jnp.float32
 NEG = -1e30
@@ -164,6 +164,13 @@
         def _():
             over_y(source(i), a, right, 2, act)
 
+    def passes(a):
+        if GIVEN:
+            @pl.when(y == 1)
+            def _():
+                over_y(2, a, left, 3, wait_recv)
+                over_y(2, a, left, 3, start)
+
     def first(i, a):
         over_y(source(i), a, right, 0, wait_recv)
         forwards(i, a, start)
@@ -255,54 +262,101 @@
     on_own(c >= 0, lambda items: causal(items, block(y, 0, k), block(y, 1, k)))
     sends(1, start)
 
-    @pl.when((k == 1) | (helper & (GIVEN > 0)))
-    def _():
-        for a in range(2):
-            over_core(y, 1 - k, a, wait_recv)
-
-    on_own(k == 1, lambda items: full(items, block(y, 0, 0), block(y, 1, 0)))
+    def help_first():
+        ask(0).wait_recv()
+        fq[0] = (fq[0].astype(F32) * LOGIT).astype(BF)
+        item = Foreign(0)
+
+        @pl.when(k == 0)
+        def _():
+            causal(
+                [item],
+                jnp.concatenate([block(3, 0, 0), block(3, 0, 1)], axis=0),
+                jnp.concatenate([block(3, 1, 0), block(3, 1, 1)], axis=0),
+            )
+
+        @pl.when(k == 1)
+        def _():
+            causal([item], block(3, 0, 0), block(3, 1, 0))
+
+        for chip in (0, 1):
+            full([item], chunk(chip, 0), chunk(chip, 1))
 
     near = y - 1
     two = (y == 3) | (helper & (GIVEN > 0))
 
-    @pl.when(chunks > 0)
-    def _():
-        first(0, 0)
-
-    @pl.when(two)
-    def _():
-        first(1, 0)
-
-    @pl.when(chunks > 0)
-    def _():
-        third(0, 0)
-
-    on_own(y > 0, lambda items: full(items, store[near, 0, 0], store[near, 1, 0]))
-
-    @pl.when(chunks > 0)
-    def _():
-        first(0, 1)
-
-    @pl.when(two)
-    def _():
-        first(1, 1)
-        third(1, 0)
-
-    on_own(y == 3, lambda items: full(items, store[0, 0, 0], store[0, 1, 0]))
-
-    @pl.when(chunks > 0)
-    def _():
-        third(0, 1)
-
-    on_own(y > 0, lambda items: full(items, store[near, 0, 1], store[near, 1, 1]))
-
-    @pl.when(two)
-    def _():
-        for a in range(2):
-            first(2, a)
-        third(1, 1)
-
-    on_own(y == 3, lambda items: full(items, store[0, 0, 1], store[0, 1, 1]))
+    def step(j, carry):
+        @pl.when((j == 0) & ((k == 1) | (helper & (GIVEN > 0))))
+        def _():
+            for a in range(2):
+                over_core(y, 1 - k, a, wait_recv)
+
+        @pl.when((j == 1) & (chunks > 0))
+        def _():
+            first(0, 0)
+
+        @pl.when((j == 1) & two)
+        def _():
+            first(1, 0)
+
+        @pl.when(j == 1)
+        def _():
+            passes(0)
+
+        @pl.when((j == 1) & (chunks > 0))
+        def _():
+            third(0, 0)
+
+        @pl.when((j == 2) & (chunks > 0))
+        def _():
+            first(0, 1)
+
+        @pl.when((j == 2) & two)
+        def _():
+            first(1, 1)
+            third(1, 0)
+
+        @pl.when(j == 2)
+        def _():
+            passes(1)
+
+        @pl.when((j == 3) & (chunks > 0))
+        def _():
+            third(0, 1)
+
+        @pl.when((j == 4) & home)
+        def _():
+            for a in range(2):
+                first(2, a)
+            third(1, 1)
+
+        if GIVEN:
+            @pl.when((j == 4) & helper)
+            def _():
+                third(1, 1)
+                help_first()
+                for a in range(2):
+                    first(2, a)
+
+        chip = jnp.where(j == 0, y, jnp.where((j == 1) | (j == 3), near, 0))
+        a_low = jnp.where(j >= 3, 1, 0)
+        a_high = jnp.where(j == 0, 1, a_low)
+        low = pl.ds(0, HALF)
+        high = pl.ds(pl.multiple_of(jnp.where(j == 0, 0, HALF), HALF), HALF)
+
+        def run(items):
+            kb, vb = (
+                jnp.concatenate([store[chip, kind, a_low, low, :], store[chip, kind, a_high, high, :]], axis=0)
+                for kind in range(2)
+            )
+            full(items, kb, vb)
+
+        on_own(
+            ((j == 0) & (k == 1)) | (((j == 1) | (j == 3)) & (y > 0)) | (((j == 2) | (j == 4)) & (y == 3)), run
+        )
+        return carry
+
+    lax.fori_loop(0, 5, step, 0)
 
     @pl.when(y == 2)
     def _():
@@ -328,27 +382,9 @@
     if GIVEN:
         @pl.when(helper)
         def _():
-            for f in range(GIVEN):
-                ask(f).wait_recv()
-                fq[f] = (fq[f].astype(F32) * LOGIT).astype(BF)
-                item = Foreign(f)
-
-                @pl.when(k == 0)
-                def _():
-                    causal(
-                        [item],
-                        jnp.concatenate([block(3, 0, 0), block(3, 0, 1)], axis=0),
-                        jnp.concatenate([block(3, 1, 0), block(3, 1, 1)], axis=0),
-                    )
-
-                @pl.when(k == 1)
-                def _():
-                    causal([item], block(3, 0, 0), block(3, 1, 0))
-
-                for chip in (0, 1, 2):
-                    full([item], chunk(chip, 0), chunk(chip, 1))
-                fout[f] = normal(facc, (7 - c) * TOK)
-                give_back(f).start()
+            full([Foreign(0)], chunk(2, 0), chunk(2, 1))
+            fout[0] = normal(facc, (7 - c) * TOK)
+            give_back(0).start()
 
     def finish(items):
         for item in items:

time: 30.1 us -> 28.9 us (0.960)
  Pallas kernels: 28.4 us -> 27.2 us
    pallas_call x1, Pallas kernels: 26.4 us -> 25.2 us  [per_device(): pl.pallas_call(kernel, out_shape=pltpu.VMEM((TOK, LH * HD), BF), in_specs...]
where the time goes in v3:
time: 28.9 us; the launch traced here: 28.8 us
  Pallas kernels  27.2 us (94%)
  between operations  1.53 us (5%)
    pallas_call x1, Pallas kernels, per_device(): pl.pallas_call(kernel, out_shape=pltpu.VMEM((TOK, LH * HD), BF), in_specs...  25.2 us
    pallas_call x1, Pallas kernels, per_device(): pl.pallas_call(hand_over, out_shape=(jax.ShapeDtypeStruct((TOK, LH * HD),...  2.03 us

profile of v3, /device:TPU:26, one launch (start us, length us, event | category | flops | bytes accessed | tf_op | source)
XLA Modules:
  0.0 28.8 jit_solution(15576003878274289935)
XLA Ops:
  1.3 0.0 copy-start
  1.3 0.0 copy-start.1
  1.3 0.0 copy-start.2
  1.3 0.0 copy-start.3
  1.3 25.2 %prefill.1.att_ref = bf16[512,1024]{1,0:T(8,128)(2,1)S(1)} custom-call(bf16[512,1024]{1,0:T(8,128)(2,1)} %q_hbm.1, bf16[512,1024]{1,0:T(8,128)(2,1)} %pk_hbm.3, bf16[512,1024]{1,0:T(8,128)(2,1)} %pv_hbm.3, s32[1]{0:T(128)S(6)} %copy.12.length_ref), custom_call_target="tpu_custom_call" | custom-call | tf_op jit(solution)/shard_map/prefill/pallas_call | solution.py:493
  26.5 0.0 copy-done
  26.5 0.0 copy-done.1
  26.5 0.0 copy-done.2
  26.5 0.0 copy-done.3
  26.6 2.0 %hand_over.1 = (bf16[512,1024]{1,0:T(8,128)(2,1)}, bf16[1,4,128,128]{3,2,1,0:T(8,128)(2,1)}, bf16[1,4,128,128]{3,2,1,0:T(8,128)(2,1)}, bf16[1,4]{1,0:T(2,128)(2,1)}, bf16[1,4]{1,0:T(2,128)(2,1)}) custom-call(bf16[512,1024]{1,0:T(8,128)(2,1)S(1)} %prefill.1.att_ref, bf16[512,1024]{1,0:T(8,128)(2,1)S(1)} %copy-done, bf16[512,1024]{1,0:T(8,128)(2,1)S(1)} %copy-done.1, ...), custom_call_target="tpu_custom_call" | custom-call | tf_op jit(solution)/shard_map/hand_over/pallas_call | solution.py:523
Async XLA Ops:
  1.3 25.2 %copy-start = (bf16[512,1024]{1,0:T(8,128)(2,1)S(1)}, bf16[512,1024]{1,0:T(8,128)(2,1)}, u32[]{:S(2)}) copy-start(bf16[512,1024]{1,0:T(8,128)(2,1)} %pk_hbm.3) | copy-start | bytes 3145732
  1.3 25.2 %copy-start.1 = (bf16[512,1024]{1,0:T(8,128)(2,1)S(1)}, bf16[512,1024]{1,0:T(8,128)(2,1)}, u32[]{:S(2)}) copy-start(bf16[512,1024]{1,0:T(8,128)(2,1)} %pv_hbm.3) | copy-start | bytes 3145732
  1.3 25.2 %copy-start.2 = (s32[4,8,1]{1,2,0:T(1,128)S(1)}, s32[4,8,1]{1,2,0:T(1,128)}, u32[]{:S(2)}) copy-start(s32[4,8,1]{1,2,0:T(1,128)} %param.9) | copy-start | bytes 388
  1.3 25.2 %copy-start.3 = (s32[8]{0:T(128)S(1)}, s32[8]{0:T(128)}, u32[]{:S(2)}) copy-start(s32[8]{0:T(128)} %layout_ref.1) | copy-start | bytes 100

commit v4 on v3

--- a/solution.py
+++ b/solution.py
@@ -97,7 +97,8 @@
 
     def own_over_y(a, device, place, act):
         for kind in range(2):
-            act(remote(raw(kind, a), piece(y, k, kind, a), y_send.at[place, kind, a], y_recv.at[y, kind, a], device))
+            ref = piece(y, k, kind, a)
+            act(remote(ref, ref, y_send.at[place, kind, a], y_recv.at[y, kind, a], device))
 
     def over_y(chip, a, device, place, act):
         for kind in range(2):
@@ -107,7 +108,8 @@
     def own_over_core(act):
         for a in range(2):
             for kind in range(2):
-                act(remote(raw(kind, a), piece(y, k, kind, a), s_send.at[y, kind, a], s_recv.at[y, kind, a], sib))
+                ref = piece(y, k, kind, a)
+                act(remote(ref, ref, s_send.at[y, kind, a], s_recv.at[y, kind, a], sib))
 
     def over_core(chip, parity, a, act):
         for kind in range(2):
@@ -118,9 +120,10 @@
         cols = pl.ds((LH - GIVEN + f) * HD, HD)
         return remote(q_hbm.at[:, cols], fq.at[f], q_send.at[f], q_recv.at[f], other_end)
 
-    def give_back(f):
-        cols = pl.ds((LH - GIVEN + f) * HD, HD)
-        return remote(fout.at[f], out_ref.at[:, cols], o_send.at[f], o_recv.at[f], other_end)
+    def give_back(part):
+        rows = pl.ds(part * HALF, HALF)
+        cols = pl.ds((LH - GIVEN) * HD, HD)
+        return remote(fout.at[0, rows], out_ref.at[rows, cols], o_send.at[part], o_recv.at[part], other_end)
 
     def start(copy):
         copy.start()
@@ -166,10 +169,8 @@
 
     def passes(a):
         if GIVEN:
-            @pl.when(y == 1)
-            def _():
-                over_y(2, a, left, 3, wait_recv)
-                over_y(2, a, left, 3, start)
+            over_y(2, a, left, 3, wait_recv)
+            over_y(2, a, left, 3, start)
 
     def first(i, a):
         over_y(source(i), a, right, 0, wait_recv)
@@ -179,15 +180,15 @@
         over_core(source(i), 1 - k, a, wait_recv)
 
     pl.semaphore_wait(barrier, len(others))
+    for copy in get_own:
+        copy.wait()
+    core_sends(start)
+    sends(0, start)
     asks(start)
-    sends(0, start)
-    core_sends(start)
 
     length = length_ref[0]
     get_q.wait()
     q_scr[...] = (q_scr[...].astype(F32) * LOGIT).astype(BF)
-    for copy in get_own:
-        copy.wait()
 
     ones = jnp.ones((2 * TOK, HD), BF)
 
@@ -206,6 +207,16 @@
         def state(self):
             return mx.at[self.h], acc.at[self.h]
 
+    class ForeignPart:
+        def __init__(self, rows):
+            self.rows = rows
+
+        def q(self):
+            return fq[0, self.rows, :]
+
+        def state(self):
+            return fmx.at[self.rows], facc.at[self.rows]
+
     class Foreign:
         def __init__(self, f):
             self.f = f
@@ -226,9 +237,9 @@
     def causal(items, kb, vb):
         before = kb.shape[0] - TOK
         vb = with_ones(vb)
-        for item in items:
-            top, total = item.state()
-            for part in range(2):
+        for part in range(2):
+            for item in items:
+                top, total = item.state()
                 rows = slice(part * HALF, (part + 1) * HALF)
                 keys = before + (part + 1) * HALF
                 s = qk(item.q(rows), kb[:keys])
@@ -299,15 +310,17 @@
         def _():
             first(1, 0)
 
-        @pl.when(j == 1)
+        @pl.when((j == 1) & (y == 1))
         def _():
             passes(0)
+            first(0, 1)
+            passes(1)
 
         @pl.when((j == 1) & (chunks > 0))
         def _():
             third(0, 0)
 
-        @pl.when((j == 2) & (chunks > 0))
+        @pl.when((j == 2) & (chunks > 0) & (y != 1))
         def _():
             first(0, 1)
 
@@ -315,10 +328,6 @@
         def _():
             first(1, 1)
             third(1, 0)
-
-        @pl.when(j == 2)
-        def _():
-            passes(1)
 
         @pl.when((j == 3) & (chunks > 0))
         def _():
@@ -377,14 +386,16 @@
 
     def normal(total, position):
         o = total[:, :HD] / total[:, HD:]
-        return jnp.where(row + position < length, o, 0.0).astype(BF)
+        return jnp.where(row[: o.shape[0]] + position < length, o, 0.0).astype(BF)
 
     if GIVEN:
         @pl.when(helper)
         def _():
-            full([Foreign(0)], chunk(2, 0), chunk(2, 1))
-            fout[0] = normal(facc, (7 - c) * TOK)
-            give_back(0).start()
+            for part in range(2):
+                rows = pl.ds(part * HALF, HALF)
+                full([ForeignPart(rows)], chunk(2, 0), chunk(2, 1))
+                fout[0, rows, :] = normal(facc.at[rows], (7 - c) * TOK + part * HALF)
+                give_back(part).start()
 
     def finish(items):
         for item in items:
@@ -398,8 +409,8 @@
 
         @pl.when(home)
         def _():
-            for f in range(GIVEN):
-                give_back(f).wait_recv()
+            for part in range(2):
+                give_back(part).wait_recv()
 
     asks(wait_send)
     for a in range(2):
@@ -421,8 +432,8 @@
 
         @pl.when(helper)
         def _():
-            for f in range(GIVEN):
-                give_back(f).wait_send()
+            for part in range(2):
+                give_back(part).wait_send()
 
 
 def hand_over(
@@ -512,8 +523,8 @@
             dma((CHIPS, 2, 2)),
             dma((given,)),
             dma((given,)),
-            dma((given,)),
-            dma((given,)),
+            dma((2,)),
+            dma((2,)),
         ],
         compiler_params=pltpu.CompilerParams(
             collective_id=0, has_side_effects=True, vmem_limit_bytes=56 << 20

time: 28.9 us -> 27.9 us (0.965)
  Pallas kernels: 27.2 us -> 26.3 us
    pallas_call x1, Pallas kernels: 25.2 us -> 24.2 us  [per_device(): pl.pallas_call(kernel, out_shape=pltpu.VMEM((TOK, LH * HD), BF), in_specs...]
where the time goes in v4:
time: 27.9 us; the launch traced here: 27.8 us
  Pallas kernels  26.3 us (94%)
  between operations  1.53 us (5%)
    pallas_call x1, Pallas kernels, per_device(): pl.pallas_call(kernel, out_shape=pltpu.VMEM((TOK, LH * HD), BF), in_specs...  24.2 us
    pallas_call x1, Pallas kernels, per_device(): pl.pallas_call(hand_over, out_shape=(jax.ShapeDtypeStruct((TOK, LH * HD),...  2.04 us

profile of v4, /device:TPU:26, one launch (start us, length us, event | category | flops | bytes accessed | tf_op | source)
XLA Modules:
  0.0 27.8 jit_solution(2448206026746859918)
XLA Ops:
  1.3 0.0 copy-start
  1.3 0.0 copy-start.1
  1.3 0.0 copy-start.2
  1.3 0.0 copy-start.3
  1.3 24.2 %prefill.1.att_ref = bf16[512,1024]{1,0:T(8,128)(2,1)S(1)} custom-call(bf16[512,1024]{1,0:T(8,128)(2,1)} %q_hbm.1, bf16[512,1024]{1,0:T(8,128)(2,1)} %pk_hbm.3, bf16[512,1024]{1,0:T(8,128)(2,1)} %pv_hbm.3, s32[1]{0:T(128)S(6)} %copy.12.length_ref), custom_call_target="tpu_custom_call" | custom-call | tf_op jit(solution)/shard_map/prefill/pallas_call | solution.py:504
  25.5 0.0 copy-done
  25.6 0.0 copy-done.1
  25.6 0.0 copy-done.2
  25.6 0.0 copy-done.3
  25.6 2.0 %hand_over.1 = (bf16[512,1024]{1,0:T(8,128)(2,1)}, bf16[1,4,128,128]{3,2,1,0:T(8,128)(2,1)}, bf16[1,4,128,128]{3,2,1,0:T(8,128)(2,1)}, bf16[1,4]{1,0:T(2,128)(2,1)}, bf16[1,4]{1,0:T(2,128)(2,1)}) custom-call(bf16[512,1024]{1,0:T(8,128)(2,1)S(1)} %prefill.1.att_ref, bf16[512,1024]{1,0:T(8,128)(2,1)S(1)} %copy-done, bf16[512,1024]{1,0:T(8,128)(2,1)S(1)} %copy-done.1, ...), custom_call_target="tpu_custom_call" | custom-call | tf_op jit(solution)/shard_map/hand_over/pallas_call | solution.py:534
Async XLA Ops:
  1.3 24.3 %copy-start = (bf16[512,1024]{1,0:T(8,128)(2,1)S(1)}, bf16[512,1024]{1,0:T(8,128)(2,1)}, u32[]{:S(2)}) copy-start(bf16[512,1024]{1,0:T(8,128)(2,1)} %pk_hbm.3) | copy-start | bytes 3145732
  1.3 24.3 %copy-start.1 = (bf16[512,1024]{1,0:T(8,128)(2,1)S(1)}, bf16[512,1024]{1,0:T(8,128)(2,1)}, u32[]{:S(2)}) copy-start(bf16[512,1024]{1,0:T(8,128)(2,1)} %pv_hbm.3) | copy-start | bytes 3145732
  1.3 24.3 %copy-start.2 = (s32[4,8,1]{1,2,0:T(1,128)S(1)}, s32[4,8,1]{1,2,0:T(1,128)}, u32[]{:S(2)}) copy-start(s32[4,8,1]{1,2,0:T(1,128)} %param.9) | copy-start | bytes 388
  1.3 24.3 %copy-start.3 = (s32[8]{0:T(128)S(1)}, s32[8]{0:T(128)}, u32[]{:S(2)}) copy-start(s32[8]{0:T(128)} %layout_ref.1) | copy-start | bytes 100

commit v5 on v4

--- a/solution.py
+++ b/solution.py
@@ -316,7 +316,7 @@
             first(0, 1)
             passes(1)
 
-        @pl.when((j == 1) & (chunks > 0))
+        @pl.when((j == 1) & (chunks > 0) & (y != 3))
         def _():
             third(0, 0)
 
@@ -329,7 +329,11 @@
             first(1, 1)
             third(1, 0)
 
-        @pl.when((j == 3) & (chunks > 0))
+        @pl.when((j == 2) & home)
+        def _():
+            third(0, 0)
+
+        @pl.when((j == 3) & (chunks > 0) & (y != 3))
         def _():
             third(0, 1)
 
@@ -337,6 +341,7 @@
         def _():
             for a in range(2):
                 first(2, a)
+            third(0, 1)
             third(1, 1)
 
         if GIVEN:
@@ -347,15 +352,18 @@
                 for a in range(2):
                     first(2, a)
 
-        chip = jnp.where(j == 0, y, jnp.where((j == 1) | (j == 3), near, 0))
+        spread = home & (j > 0)
+        chip = jnp.where(j == 0, y, near)
+        chip_high = jnp.where(spread, 0, chip)
         a_low = jnp.where(j >= 3, 1, 0)
         a_high = jnp.where(j == 0, 1, a_low)
-        low = pl.ds(0, HALF)
-        high = pl.ds(pl.multiple_of(jnp.where(j == 0, 0, HALF), HALF), HALF)
+        parity = jnp.where((j == 1) | (j == 3), k, 1 - k)
+        low = pl.ds(pl.multiple_of(jnp.where(spread, parity, 0) * HALF, HALF), HALF)
+        high = pl.ds(pl.multiple_of(jnp.where(spread, parity, jnp.where(j == 0, 0, 1)) * HALF, HALF), HALF)
 
         def run(items):
             kb, vb = (
-                jnp.concatenate([store[chip, kind, a_low, low, :], store[chip, kind, a_high, high, :]], axis=0)
+                jnp.concatenate([store[chip, kind, a_low, low, :], store[chip_high, kind, a_high, high, :]], axis=0)
                 for kind in range(2)
             )
             full(items, kb, vb)

time: 27.9 us -> 27.8 us (level)
  no operation moved by 1% of the time
where the time goes in v5:
time: 27.8 us; the launch traced here: 27.7 us
  Pallas kernels  26.2 us (94%)
  between operations  1.53 us (6%)
    pallas_call x1, Pallas kernels, per_device(): pl.pallas_call(kernel, out_shape=pltpu.VMEM((TOK, LH * HD), BF), in_specs...  24.1 us
    pallas_call x1, Pallas kernels, per_device(): pl.pallas_call(hand_over, out_shape=(jax.ShapeDtypeStruct((TOK, LH * HD),...  2.04 us

profile of v5, /device:TPU:26, one launch (start us, length us, event | category | flops | bytes accessed | tf_op | source)
XLA Modules:
  0.0 27.7 jit_solution(366031371168931055)
XLA Ops:
  1.3 0.0 copy-start
  1.3 0.0 copy-start.1
  1.3 0.0 copy-start.2
  1.3 0.0 copy-start.3
  1.3 24.1 %prefill.1.att_ref = bf16[512,1024]{1,0:T(8,128)(2,1)S(1)} custom-call(bf16[512,1024]{1,0:T(8,128)(2,1)} %q_hbm.1, bf16[512,1024]{1,0:T(8,128)(2,1)} %pk_hbm.3, bf16[512,1024]{1,0:T(8,128)(2,1)} %pv_hbm.3, s32[1]{0:T(128)S(6)} %copy.12.length_ref), custom_call_target="tpu_custom_call" | custom-call | tf_op jit(solution)/shard_map/prefill/pallas_call | solution.py:512
  25.4 0.0 copy-done
  25.5 0.0 copy-done.1
  25.5 0.0 copy-done.2
  25.5 0.0 copy-done.3
  25.5 2.0 %hand_over.1 = (bf16[512,1024]{1,0:T(8,128)(2,1)}, bf16[1,4,128,128]{3,2,1,0:T(8,128)(2,1)}, bf16[1,4,128,128]{3,2,1,0:T(8,128)(2,1)}, bf16[1,4]{1,0:T(2,128)(2,1)}, bf16[1,4]{1,0:T(2,128)(2,1)}) custom-call(bf16[512,1024]{1,0:T(8,128)(2,1)S(1)} %prefill.1.att_ref, bf16[512,1024]{1,0:T(8,128)(2,1)S(1)} %copy-done, bf16[512,1024]{1,0:T(8,128)(2,1)S(1)} %copy-done.1, ...), custom_call_target="tpu_custom_call" | custom-call | tf_op jit(solution)/shard_map/hand_over/pallas_call | solution.py:542
Async XLA Ops:
  1.3 24.2 %copy-start = (bf16[512,1024]{1,0:T(8,128)(2,1)S(1)}, bf16[512,1024]{1,0:T(8,128)(2,1)}, u32[]{:S(2)}) copy-start(bf16[512,1024]{1,0:T(8,128)(2,1)} %pk_hbm.3) | copy-start | bytes 3145732
  1.3 24.2 %copy-start.1 = (bf16[512,1024]{1,0:T(8,128)(2,1)S(1)}, bf16[512,1024]{1,0:T(8,128)(2,1)}, u32[]{:S(2)}) copy-start(bf16[512,1024]{1,0:T(8,128)(2,1)} %pv_hbm.3) | copy-start | bytes 3145732
  1.3 24.2 %copy-start.2 = (s32[4,8,1]{1,2,0:T(1,128)S(1)}, s32[4,8,1]{1,2,0:T(1,128)}, u32[]{:S(2)}) copy-start(s32[4,8,1]{1,2,0:T(1,128)} %param.9) | copy-start | bytes 388
  1.3 24.2 %copy-start.3 = (s32[8]{0:T(128)S(1)}, s32[8]{0:T(128)}, u32[]{:S(2)}) copy-start(s32[8]{0:T(128)} %layout_ref.1) | copy-start | bytes 100
